TPU v7x, 32 devices: a whole 2x2x4 slice. The times are simulated.
32 devices in a mesh: slide: 8 (over z, x), rep: 4 (over y, core).
Axes of the slice: x: 2, y: 2, z: 4, core: 2. Of those that a mesh axis runs over, the one named last changes fastest.
Arguments:
- tile_feats: bfloat16 [128, 8, 8, 192], P(('slide', 'rep'))
- cotangent: bfloat16 [128, 4, 4, 384], P(('slide', 'rep')), may hold values from -0.125 to 0.125
- keep_list: int32 [32, 4], P(('slide', 'rep')), may hold values from 0 to 3, each once within a row
- tile_plan: int32 [32, 2], P(('slide', 'rep')), may hold values from 0 to 4, as said below
- kernel_one: bfloat16 [7, 7, 192], replicated, may hold values from -0.875 to 0.875
- gain_one: bfloat16 [192], replicated, may hold values from 0.25 to 1.75
- inward_one: bfloat16 [192, 768], replicated, may hold values from -0.4375 to 0.4375
- outward_one: bfloat16 [768, 192], replicated, may hold values from -0.21875 to 0.21875
- gain_down: bfloat16 [192], replicated, may hold values from 0.25 to 1.75
- project_down: bfloat16 [768, 384], replicated, may hold values from -0.21875 to 0.21875
- kernel_two: bfloat16 [7, 7, 384], replicated, may hold values from -0.875 to 0.875
- gain_two: bfloat16 [384], replicated, may hold values from 0.25 to 1.75
- inward_two: bfloat16 [384, 1536], replicated, may hold values from -0.3125 to 0.3125
- outward_two: bfloat16 [1536, 384], replicated, may hold values from -0.15625 to 0.15625
Outputs:
- features: bfloat16 [128, 4, 4, 384], P(('slide', 'rep'))
- grad_inward: float32 [192, 768], P(None, 'slide')
- grad_outward: float32 [768, 192], P('slide')
- grad_project: float32 [768, 384], P('slide')
Inputs may be any that keep to these rules, and one draw needn't show every extreme that they name: `keep_list`: each row is a permutation of 0 to 3. `tile_plan`: column 0 counts the device's kept tiles, column 1 is its partner bit, from 0 to 2. The device at the same rep index whose slide index differs only in that bit is its partner and has the same partner bit; the bit is the same over each aligned group of 8 slide indices. Partners' counts sum to at most 4. In every replica some device keeps 4 tiles and its partner none.
All inputs are finite; a program needn't handle non-finite values.
Results may differ from a plain program's by a relative error of at most 0.018.
Values may be sent and summed in bfloat16 or wider, within the bound.
A program may use at most 64 MiB of HBM per device.

v0:
```python
import jax
import jax.numpy as jnp
from jax import lax
from jax.sharding import PartitionSpec as P


def depthwise(field, kernel):
    return lax.conv_general_dilated(
        field.astype(jnp.float32),
        kernel.astype(jnp.float32)[:, :, None, :],
        (1, 1),
        "SAME",
        dimension_numbers=("NHWC", "HWIO", "NHWC"),
        feature_group_count=field.shape[-1],
        precision=lax.Precision.HIGHEST,
    )


def layer_norm(values, gain):
    centre = jnp.mean(values, axis=-1, keepdims=True)
    offset = values - centre
    spread = jnp.mean(offset * offset, axis=-1, keepdims=True)
    return offset * lax.rsqrt(spread + 1e-06) * gain.astype(jnp.float32)


def gelu_exact(values):
    return jax.nn.gelu(values, approximate=False)


def slot_pass(tile_feats, cotangent, weights):
    (
        kernel_one,
        gain_one,
        inward_one,
        outward_one,
        gain_down,
        project_down,
        kernel_two,
        gain_two,
        inward_two,
        outward_two,
    ) = weights
    slot_count = tile_feats.shape[0]
    side_cells = tile_feats.shape[1]
    narrow_width = tile_feats.shape[3]
    half_side = side_cells // 2
    wide_width = project_down.shape[1]
    first_rows = slot_count * side_cells * side_cells
    second_rows = slot_count * half_side * half_side
    normed = (
        layer_norm(depthwise(tile_feats, kernel_one), gain_one)
        .astype(jnp.bfloat16)
        .reshape(first_rows, narrow_width)
    )
    expand = jnp.dot(normed, inward_one, preferred_element_type=jnp.float32)
    hidden = gelu_exact(expand).astype(jnp.bfloat16)
    flat_input = tile_feats.reshape(first_rows, narrow_width)
    section_one = (
        flat_input.astype(jnp.float32)
        + jnp.dot(hidden, outward_one, preferred_element_type=jnp.float32)
    ).astype(jnp.bfloat16)
    down_normed = layer_norm(section_one.astype(jnp.float32), gain_down).astype(jnp.bfloat16)
    patches = (
        down_normed.reshape(slot_count, half_side, 2, half_side, 2, narrow_width)
        .transpose(0, 1, 3, 2, 4, 5)
        .reshape(second_rows, 4 * narrow_width)
    )
    merged = jnp.dot(patches, project_down, preferred_element_type=jnp.float32).astype(jnp.bfloat16)
    merged_grid = merged.reshape(slot_count, half_side, half_side, wide_width).astype(jnp.float32)

    def second_norm(values):
        return layer_norm(depthwise(values, kernel_two), gain_two)

    normed_two = second_norm(merged_grid).astype(jnp.bfloat16).reshape(second_rows, wide_width)
    expand_two = jnp.dot(normed_two, inward_two, preferred_element_type=jnp.float32)
    hidden_two = gelu_exact(expand_two).astype(jnp.bfloat16)
    features = (
        merged.astype(jnp.float32)
        + jnp.dot(hidden_two, outward_two, preferred_element_type=jnp.float32)
    ).astype(jnp.bfloat16)
    flat_cot = cotangent.reshape(second_rows, wide_width)
    back_hidden_two = jnp.dot(flat_cot, outward_two.T, preferred_element_type=jnp.float32).astype(
        jnp.bfloat16
    )
    unused, gelu_back_two = jax.vjp(gelu_exact, expand_two)
    back_expand_two = gelu_back_two(back_hidden_two.astype(jnp.float32))[0].astype(jnp.bfloat16)
    back_normed_two = jnp.dot(
        back_expand_two, inward_two.T, preferred_element_type=jnp.float32
    ).astype(jnp.bfloat16)
    unused, norm_back_two = jax.vjp(second_norm, merged_grid)
    back_depth = norm_back_two(
        back_normed_two.astype(jnp.float32).reshape(slot_count, half_side, half_side, wide_width)
    )[0]
    back_merged = (
        flat_cot.astype(jnp.float32) + back_depth.reshape(second_rows, wide_width)
    ).astype(jnp.bfloat16)
    grad_project = jnp.dot(patches.T, back_merged, preferred_element_type=jnp.float32)
    back_patches = jnp.dot(back_merged, project_down.T, preferred_element_type=jnp.float32).astype(
        jnp.bfloat16
    )
    back_down = (
        back_patches.reshape(slot_count, half_side, half_side, 2, 2, narrow_width)
        .transpose(0, 1, 3, 2, 4, 5)
        .reshape(first_rows, narrow_width)
    )
    unused, norm_back_down = jax.vjp(
        lambda values: layer_norm(values, gain_down), section_one.astype(jnp.float32)
    )
    back_section = norm_back_down(back_down.astype(jnp.float32))[0].astype(jnp.bfloat16)
    grad_outward = jnp.dot(hidden.T, back_section, preferred_element_type=jnp.float32)
    back_hidden = jnp.dot(back_section, outward_one.T, preferred_element_type=jnp.float32).astype(
        jnp.bfloat16
    )
    unused, gelu_back = jax.vjp(gelu_exact, expand)
    back_expand = gelu_back(back_hidden.astype(jnp.float32))[0].astype(jnp.bfloat16)
    grad_inward = jnp.dot(normed.T, back_expand, preferred_element_type=jnp.float32)
    return (
        features.reshape(slot_count, half_side, half_side, wide_width),
        grad_inward,
        grad_outward,
        grad_project,
    )


def column_mask(mask, rank):
    return mask.reshape(mask.shape + (1,) * rank)


def per_device(
    tile_feats,
    cotangent,
    keep_list,
    tile_plan,
    kernel_one,
    gain_one,
    inward_one,
    outward_one,
    gain_down,
    project_down,
    kernel_two,
    gain_two,
    inward_two,
    outward_two,
):
    weights = (
        kernel_one,
        gain_one,
        inward_one,
        outward_one,
        gain_down,
        project_down,
        kernel_two,
        gain_two,
        inward_two,
        outward_two,
    )
    candidates = tile_feats.shape[0]
    ordering = keep_list[0]
    kept_count = tile_plan[0, 0]
    positions = jnp.arange(candidates, dtype=jnp.int32)
    live = positions < kept_count
    zero_value = jnp.zeros((), jnp.bfloat16)
    ordered_tiles = jnp.where(column_mask(live, 3), tile_feats[ordering], zero_value)
    ordered_cot = jnp.where(column_mask(live, 3), cotangent[ordering], zero_value)
    position_feats, grad_inward, grad_outward, grad_project = slot_pass(
        ordered_tiles, ordered_cot, weights
    )
    place = jnp.sum(
        jnp.where(ordering[None, :] == positions[:, None], positions[None, :], 0), axis=1
    )
    features = jnp.where(column_mask(place < kept_count, 3), position_feats[place], zero_value)
    totals = lax.psum((grad_inward, grad_outward, grad_project), ("slide", "rep"))
    where_index = lax.axis_index("slide")
    parts_count = lax.axis_size("slide")
    span_columns = grad_inward.shape[1] // parts_count
    span_rows = grad_outward.shape[0] // parts_count
    span_project = grad_project.shape[0] // parts_count
    inward_share = lax.dynamic_slice_in_dim(totals[0], where_index * span_columns, span_columns, 1)
    outward_share = lax.dynamic_slice_in_dim(totals[1], where_index * span_rows, span_rows, 0)
    project_share = lax.dynamic_slice_in_dim(totals[2], where_index * span_project, span_project, 0)
    return (features, inward_share, outward_share, project_share)


def solution(mesh):
    in_specs = (
        P(("slide", "rep"), None, None, None),
        P(("slide", "rep"), None, None, None),
        P(("slide", "rep"), None),
        P(("slide", "rep"), None),
        P(),
        P(),
        P(),
        P(),
        P(),
        P(),
        P(),
        P(),
        P(),
        P(),
    )
    out_specs = (
        P(("slide", "rep"), None, None, None),
        P(None, "slide"),
        P("slide", None),
        P("slide", None),
    )
    return jax.shard_map(
        per_device, mesh=mesh, in_specs=in_specs, out_specs=out_specs, check_vma=False
    )
```

profile of v0, /device:TPU:0, one launch (start us, length us, event | category | flops | bytes accessed | tf_op | source)
XLA Modules:
  0.0 188.0 jit_solution(13950664272120194174)
XLA Ops:
  7.2 0.9 select_reduce_fusion
  8.1 1.2 fusion.44
  9.3 1.2 iota_compare_fusion.1
  10.5 0.7 convert_element_type.105
  11.2 1.5 gather_fusion
  12.7 2.2 %fusion.61 = (f32[4,8,8]{0,2,1:T(8,128)S(1)}, f32[4,8,8,192]{3,0,2,1:T(4,128)S(1)}) fusion(bf16[7,7,1,192]{3,1,0,2:T(8,128)(2,1)} %bitcast.46, bf16[4,8,8,192]{3,2,1,0:T(8,128)(2,1)S(1)} %broadcast_select_fusion), kind=kOutput, calls=%fused_computation.129 | convolution fusion | flops 3022592 | bytes 314752 | tf_op jit(solution)/shard_map/conv_general_dilated | solution.py:8
  15.0 0.3 multiply_reduce_fusion
  15.3 0.2 multiply_convert_fusion.2
  15.5 0.1 copy.44
  15.7 0.1 broadcast_in_dim.104
  15.8 2.9 %multiply_convert_fusion = (bf16[256,768]{1,0:T(8,128)(2,1)S(1)}, f32[256,768]{1,0:T(8,128)}, f32[256,768]{1,0:T(8,128)}) fusion(bf16[256,192]{1,0:T(8,128)(2,1)S(1)} %bitcast.40, bf16[192,768]{1,0:T(8,128)(2,1)S(1)} %copy-done.16), kind=kOutput, calls=%fused_computation.21 | convolution fusion | flops 88276992 | bytes 2359296 | tf_op jit(solution)/shard_map/dot_general | solution.py:55
  18.7 0.3 fusion.62
  19.1 0.6 copy-done.9
  19.7 0.1 multiply_convert_fusion.4
  19.8 0.1 copy.48
  20.0 0.1 copy.49
  20.1 0.1 reshape.169
  20.2 0.2 convolution_convert_fusion.4
  20.5 0.6 fusion.63
  21.2 0.2 multiply_reduce_fusion.4
  21.4 0.1 multiply_convert_fusion.5
  21.5 0.6 gather_fusion.2
  22.2 0.1 broadcast_in_dim.113
  22.4 0.3 fusion.64
  22.7 3.2 %fusion.6 = f32[64,384]{1,0:T(8,128)} fusion(bf16[384,1536]{1,0:T(8,128)(2,1)S(1)} %copy-done, bf16[1536,384]{1,0:T(8,128)(2,1)} %param.27, f32[64,1536]{1,0:T(8,128)S(1)} %fusion.64, bf16[64,384]{1,0:T(8,128)(2,1)S(1)} %gather.17, pred[64]{0:T(512)(128)(4,1)S(1)} %broadcast_in_dim.113), kind=kOutput, calls=%fused_computation.16 | convolution fusion | flops 158343168 | bytes 2900032 | tf_op jit(solution)/shard_map/dot_general | solution.py:87
  25.9 0.9 reshape.177
  26.9 0.2 multiply_reduce_fusion.3
  27.1 0.2 fusion.56
  27.3 2.0 %add_convert_fusion.3 = (bf16[4,4,4,384]{3,0,2,1:T(4,128)(2,1)}, f32[4,4,4,384]{3,0,2,1:T(4,128)S(1)}) fusion(bf16[4,4,4,384]{3,2,1,0:T(4,128)(2,1)S(1)} %gather_fusion.2, pred[4]{0:T(512)(128)(4,1)S(1)} %get-tuple-element.34, bf16[7,7,384,1]{2,1,0,3:T(8,128)(2,1)} %bitcast.44, f32[4,4,4]{0,2,1:T(4,128)S(1)} %negate_multiply_fusion.4, ...), kind=kOutput, calls=%fused_computation.76 | convolution fusion | flops 4988928 | bytes 433412 | tf_op jit(solution)/shard_map/transpose(jvp())/conv_general_dilated | solution.py:8
  29.4 0.9 fusion.4
  30.4 0.2 reshape.179
  30.7 0.2 reshape.178
  30.9 0.1 copy.58
  31.0 0.1 multiply_reduce_fusion.1
  31.1 0.1 fusion.59
  31.3 0.2 copy-done.6
  31.5 1.4 fusion.65
  32.8 1.2 fusion.41
  34.0 2.8 %fusion.8 = f32[192,768]{1,0:T(8,128)} fusion(bf16[256,192]{1,0:T(8,128)(2,1)S(1)} %bitcast.41, f32[256,768]{1,0:T(8,128)} %get-tuple-element.22, bf16[768,192]{0,1:T(8,128)(2,1)S(1)} %copy-done.2, f32[256,768]{1,0:T(8,128)} %get-tuple-element.25, f32[256,192]{0,1:T(8,128)S(1)} %get-tuple-element.20, f32[256]{0:T(256)S(1)} %negate_multiply_fusion.5), kind=kOutput, calls=%fused_computation.20 | convolution fusion | flops 154238976 | bytes 2753536 | tf_op jit(solution)/shard_map/dot_general | solution.py:116
  36.9 1.2 copy-done.15
  38.1 1.0 fusion.5
  39.2 0.6 gather_fusion.1
  39.8 0.1 copy_select_fusion.1
  39.9 0.6 copy.61
  40.5 135.9 %all-reduce.3.cloned.1.call-done = (f32[192,768]{1,0:T(8,128)}, f32[768,192]{1,0:T(8,128)}, f32[768,384]{1,0:T(8,128)}) async-done(((f32[192,768]{1,0:T(8,128)}, f32[768,192]{1,0:T(8,128)}, f32[768,384]{1,0:T(8,128)}), (f32[192,768]{1,0:T(8,128)}, f32[768,192]{1,0:T(8,128)}, f32[768,384]{1,0:T(8,128)})) %all-reduce.3.cloned.1.call-update) | async-done | bytes 2359312 | tf_op jit(solution)/shard_map/psum | solution.py:172
  176.4 1.7 constant_dynamic-slice_fusion.1
  178.0 1.5 constant_dynamic-slice_fusion
  179.6 1.6 constant_dynamic-slice_fusion.2
  (67 shorter events, 0.9 us)
Async XLA Ops:
  7.2 15.2 %copy-start = (bf16[384,1536]{1,0:T(8,128)(2,1)S(1)}, bf16[384,1536]{1,0:T(8,128)(2,1)}, u32[]{:S(2)}) copy-start(bf16[384,1536]{1,0:T(8,128)(2,1)} %param.26) | copy-start | bytes 3538948
  7.2 169.2 %all-reduce.3.cloned.1.call-start = ((), (), s32[]{:S(2)}) async-start(), calls=%async_computation | async-start | bytes 5111808 | tf_op jit(solution)/shard_map/psum | solution.py:172
  12.6 3.2 %copy-start.18 = (bf16[192]{0:T(256)(128)(2,1)S(1)}, bf16[192]{0:T(256)(128)(2,1)}, u32[]{:S(2)}) copy-start(bf16[192]{0:T(256)(128)(2,1)} %param.22) | copy-start | bytes 1156
  12.6 3.2 %copy-start.16 = (bf16[192,768]{1,0:T(8,128)(2,1)S(1)}, bf16[192,768]{1,0:T(8,128)(2,1)}, u32[]{:S(2)}) copy-start(bf16[192,768]{1,0:T(8,128)(2,1)} %param.20) | copy-start | bytes 884740
  15.5 3.2 %copy-start.3 = (bf16[4,8,8,192]{3,2,1,0:T(8,128)(2,1)}, bf16[4,8,8,192]{3,2,1,0:T(8,128)(2,1)S(1)}, u32[]{:S(2)}) copy-start(bf16[4,8,8,192]{3,2,1,0:T(8,128)(2,1)S(1)} %copy.47) | copy-start | bytes 294916
  15.8 2.9 %copy-start.2 = (bf16[768,192]{0,1:T(8,128)(2,1)S(1)}, bf16[768,192]{0,1:T(8,128)(2,1)}, u32[]{:S(2)}) copy-start(bf16[768,192]{0,1:T(8,128)(2,1)} %param.21) | copy-start | bytes 884740
  18.7 1.5 copy-start.1
  19.0 1.5 copy-start.14
  19.0 1.5 copy-start.17
  19.1 0.6 copy-start.9
  19.7 0.8 copy-start.7
  20.0 1.6 copy-start.5
  22.4 3.6 %copy-start.11 = (pred[64]{0:T(512)(128)(4,1)}, pred[64]{0:T(512)(128)(4,1)S(1)}, u32[]{:S(2)}) copy-start(pred[64]{0:T(512)(128)(4,1)S(1)} %broadcast_in_dim.113) | copy-start | bytes 196
  30.3 0.8 copy-start.10
  30.4 0.8 copy-start.8
  30.6 0.8 copy-start.6
  31.5 2.6 %copy-start.4 = (bf16[4,8,8,192]{3,2,1,0:T(8,128)(2,1)S(1)}, bf16[4,8,8,192]{3,2,1,0:T(8,128)(2,1)}, u32[]{:S(2)}) copy-start(bf16[4,8,8,192]{3,2,1,0:T(8,128)(2,1)} %copy-done.3) | copy-start | bytes 294916
  36.9 1.3 copy-start.15
  38.1 1.0 copy-start.13
  38.1 1.6 copy-start.12
Sparse Core Ops, SparseCore 0:
  37.0 139.3 all-reduce.2
where the time goes:
time: 189 us; the launch traced here: 188 us
  waiting for transfers between devices  136 us (72%)
  matrix products  19.1 us (10%)
  between operations  14.5 us (8%)
  local copies, waits for them, and re-layouts  12.7 us (7%)
  other arithmetic  5.74 us (3%)
    psum x1, waiting for transfers between devices, per_device(): lax.psum((grad_inward, grad_outward, grad_project), ('slide', 'rep'))  136 us
    conv_general_dilated x3, matrix products, depthwise(): lax.conv_general_dilated(field.astype(jnp.float32), kernel.astype(jnp.flo...  4.9 us
  transfers between devices with their start and end apart: 1, of which 1 were waited for; matrix products, arithmetic and copies ran while one was open for 1% of the time, Pallas kernels for 0%

commit v1 on v0

--- a/solution.py
+++ b/solution.py
@@ -1,6 +1,10 @@
+import functools
+
 import jax
 import jax.numpy as jnp
 from jax import lax
+from jax.experimental import pallas as pl
+from jax.experimental.pallas import tpu as pltpu
 from jax.sharding import PartitionSpec as P
 
 
@@ -113,13 +117,128 @@
     )
     unused, gelu_back = jax.vjp(gelu_exact, expand)
     back_expand = gelu_back(back_hidden.astype(jnp.float32))[0].astype(jnp.bfloat16)
-    grad_inward = jnp.dot(normed.T, back_expand, preferred_element_type=jnp.float32)
+    grad_inward = jnp.dot(back_expand.T, normed, preferred_element_type=jnp.float32)
     return (
         features.reshape(slot_count, half_side, half_side, wide_width),
         grad_inward,
         grad_outward,
         grad_project,
     )
+
+
+MESH = pl.DeviceIdType.MESH
+
+
+def exchange_kernel(line, halves, out, get_pair, put_quad, get_quad, mine, put_line, get_line, put_rep, get_rep, pair_sems, quad_sems, line_sems, rep_sems):
+    s = lax.axis_index("slide")
+    r = lax.axis_index("rep")
+    core, y = r % 2, r // 2
+    x, z = s % 2, s // 2
+    spot = x * 2 + y
+    pair_peer = (s, y * 2 + 1 - core)
+
+    def quad_peer(d):
+        return (z * 2 + (x + d // 2) % 2, ((y + d) % 2) * 2 + core)
+
+    def line_peer(d):
+        return (((z + d) % line) * 2 + x, r)
+
+    def rep_peer(d):
+        return (s, ((y + d // 2) % 2) * 2 + (core + d) % 2)
+
+    def quad_spot(d):
+        return ((x + d // 2) % 2) * 2 + (y + d) % 2
+
+    barrier = pltpu.get_barrier_semaphore()
+    peers = [rep_peer(d) for d in (1, 2, 3)] + [quad_peer(d) for d in (2, 3)] + [line_peer(d) for d in range(1, line)]
+    for peer in peers:
+        pl.semaphore_signal(barrier, inc=1, device_id=peer, device_id_type=MESH)
+    pl.semaphore_wait(barrier, len(peers))
+
+    def send(src, dst, sems, slot, peer):
+        copy = pltpu.make_async_remote_copy(
+            src_ref=src, dst_ref=dst, send_sem=sems.at[0, slot], recv_sem=sems.at[1, slot],
+            device_id=peer, device_id_type=MESH)
+        copy.start()
+        return copy
+
+    pairs = {}
+    for d in (3, 2, 1, 0):
+        pairs[d] = send(halves.at[1 - core, quad_spot(d)], get_pair.at[d], pair_sems, d, pair_peer)
+    quads = {}
+    for d in (3, 2, 1):
+        pairs[d].wait_recv()
+        put_quad[d - 1] = (halves[core, quad_spot(d)].astype(jnp.float32) + get_pair[d].astype(jnp.float32)).astype(jnp.bfloat16)
+        quads[d] = send(put_quad.at[d - 1], get_quad.at[d - 1], quad_sems, d - 1, quad_peer(d))
+    pairs[0].wait_recv()
+    mine[...] = halves[core, spot].astype(jnp.float32) + get_pair[0].astype(jnp.float32)
+    for d in (1, 2, 3):
+        quads[d].wait_recv()
+    lines = {}
+    for d in [*range(line - 1, 0, -1), 0]:
+        at = (z + d) % line
+        part = mine[at] + get_quad[0, at].astype(jnp.float32) + get_quad[1, at].astype(jnp.float32) + get_quad[2, at].astype(jnp.float32)
+        if d:
+            put_line[d - 1] = part.astype(jnp.bfloat16)
+            lines[d] = send(put_line.at[d - 1], get_line.at[d - 1], line_sems, d - 1, line_peer(d))
+        else:
+            total = part
+    for d in range(1, line):
+        lines[d].wait_recv()
+        total = total + get_line[d - 1].astype(jnp.float32)
+    put_rep[...] = total.astype(jnp.bfloat16)
+    reps = {}
+    for d in (3, 2, 1):
+        reps[d] = send(put_rep, get_rep.at[d - 1], rep_sems, d - 1, rep_peer(d))
+    out[core, y] = put_rep[...].astype(jnp.float32)
+    for d in (1, 3, 2):
+        reps[d].wait_recv()
+        out[(core + d) % 2, (y + d // 2) % 2] = get_rep[d - 1].astype(jnp.float32)
+    for copy in [*pairs.values(), *quads.values(), *lines.values(), *reps.values()]:
+        copy.wait_send()
+
+
+def exchange(halves, slides):
+    line = slides // 2
+    block = halves.shape[-2:]
+    return pl.pallas_call(
+        functools.partial(exchange_kernel, line),
+        out_shape=jax.ShapeDtypeStruct((2, 2) + block, jnp.float32),
+        in_specs=[pl.BlockSpec(memory_space=pltpu.VMEM)],
+        out_specs=pl.BlockSpec(memory_space=pltpu.VMEM),
+        scratch_shapes=[
+            pltpu.VMEM((4, line) + block, jnp.bfloat16),
+            pltpu.VMEM((3, line) + block, jnp.bfloat16),
+            pltpu.VMEM((3, line) + block, jnp.bfloat16),
+            pltpu.VMEM((line,) + block, jnp.float32),
+            pltpu.VMEM((line - 1,) + block, jnp.bfloat16),
+            pltpu.VMEM((line - 1,) + block, jnp.bfloat16),
+            pltpu.VMEM(block, jnp.bfloat16),
+            pltpu.VMEM((3,) + block, jnp.bfloat16),
+            pltpu.SemaphoreType.DMA((2, 4)),
+            pltpu.SemaphoreType.DMA((2, 3)),
+            pltpu.SemaphoreType.DMA((2, line - 1)),
+            pltpu.SemaphoreType.DMA((2, 3)),
+        ],
+        compiler_params=pltpu.CompilerParams(collective_id=0, has_side_effects=True, vmem_limit_bytes=48 * 1024 * 1024),
+        cost_estimate=pl.CostEstimate(flops=10**6, bytes_accessed=4 * 10**6, transcendentals=0),
+    )(halves)
+
+
+def shares(grad_inward_t, grad_outward, grad_project):
+    slides, reps = lax.axis_size("slide"), lax.axis_size("rep")
+    rows, narrow = grad_outward.shape
+    both = jnp.concatenate([grad_inward_t, grad_outward], axis=1)
+    if reps == 4 and slides % 2 == 0 and slides > 2 and rows % (slides * 32) == 0 and both.shape == grad_project.shape:
+        line, part = slides // 2, rows // slides // 2
+        halves = jnp.stack([grad_project, both]).astype(jnp.bfloat16)
+        halves = halves.reshape(2, line, 4, part, -1).transpose(0, 2, 1, 3, 4)
+        got = exchange(halves, slides).reshape(2, 2 * part, -1)
+        project, both = got[0], got[1]
+    else:
+        project, both = (
+            lax.psum(lax.psum_scatter(g, "slide", scatter_dimension=0, tiled=True), "rep") for g in (grad_project, both))
+    return both[:, :narrow].T, both[:, narrow:], project
 
 
 def column_mask(mask, rank):
@@ -169,15 +288,7 @@
         jnp.where(ordering[None, :] == positions[:, None], positions[None, :], 0), axis=1
     )
     features = jnp.where(column_mask(place < kept_count, 3), position_feats[place], zero_value)
-    totals = lax.psum((grad_inward, grad_outward, grad_project), ("slide", "rep"))
-    where_index = lax.axis_index("slide")
-    parts_count = lax.axis_size("slide")
-    span_columns = grad_inward.shape[1] // parts_count
-    span_rows = grad_outward.shape[0] // parts_count
-    span_project = grad_project.shape[0] // parts_count
-    inward_share = lax.dynamic_slice_in_dim(totals[0], where_index * span_columns, span_columns, 1)
-    outward_share = lax.dynamic_slice_in_dim(totals[1], where_index * span_rows, span_rows, 0)
-    project_share = lax.dynamic_slice_in_dim(totals[2], where_index * span_project, span_project, 0)
+    inward_share, outward_share, project_share = shares(grad_inward, grad_outward, grad_project)
     return (features, inward_share, outward_share, project_share)
 
 

time: 189 us -> 64.7 us (0.34)
  waiting for transfers between devices: 136 us -> 0 us
  Pallas kernels: 0 us -> 24.1 us
  between operations: 14.5 us -> 1.2 us
  other arithmetic: 5.74 us -> 9.34 us
  matrix products: 19.1 us -> 15.7 us
    psum x1 -> x0, waiting for transfers between devices: 136 us -> none  [per_device(): lax.psum((grad_inward, grad_outward, grad_project), ('slide', 'rep'))]
    pallas_call x0 -> x1, Pallas kernels: none -> 24.1 us  [exchange(): pl.pallas_call(functools.partial(exchange_kernel, line), out_shape=jax.Sh...]
    dynamic_slice x3 -> x0, local copies, waits for them, and re-layouts: 4.78 us -> none  [the longest x1 1.66 us: per_device(): lax.dynamic_slice_in_dim(totals[0], where_index * span_columns, span_colu...]
    unnamed x39 -> x52, local copies, waits for them, and re-layouts: 2.7 us -> 4.35 us
  transfers between devices with their start and end apart: 1 -> 0, of which waited for: 1 -> 0; matrix products, arithmetic and copies ran while one was open for 1% -> 0% of each run, Pallas kernels for 0% -> 0%
where the time goes in v1:
time: 64.7 us; the launch traced here: 64.1 us
  Pallas kernels  24.1 us (37%)
  matrix products  15.7 us (24%)
  local copies, waits for them, and re-layouts  13.6 us (21%)
  other arithmetic  9.34 us (14%)
  between operations  1.2 us (2%)
    pallas_call x1, Pallas kernels, exchange(): pl.pallas_call(functools.partial(exchange_kernel, line), out_shape=jax.Sh...  24.1 us
    unnamed x52, local copies, waits for them, and re-layouts  4.35 us
    conv_general_dilated x3, matrix products, depthwise(): lax.conv_general_dilated(field.astype(jnp.float32), kernel.astype(jnp.flo...  4.3 us
    dot_general x1, matrix products, slot_pass(): jnp.dot(back_expand_two, inward_two.T, preferred_element_type=jnp.float32)  3.25 us
    dot_general x1, matrix products, slot_pass(): expand = jnp.dot(normed, inward_one, preferred_element_type=jnp.float32)  2.86 us
    dot_general x1, matrix products, slot_pass(): jnp.dot(back_expand.T, normed, preferred_element_type=jnp.float32)  2.02 us
    convert_element_type x3, other arithmetic, layer_norm(): return offset * lax.rsqrt(spread + 1e-06) * gain.astype(jnp.float32)  2 us
    dot_general x1, matrix products, slot_pass(): jnp.dot(hidden_two, outward_two, preferred_element_type=jnp.float32)  1.61 us

profile of v1, /device:TPU:0, one launch (start us, length us, event | category | flops | bytes accessed | tf_op | source)
XLA Modules:
  0.0 64.1 jit_solution(11306014959359163314)
XLA Ops:
  0.6 0.9 %select_reduce_fusion = s32[4]{0:T(128)S(1)} fusion(s32[4]{0:T(128)} %bitcast.61), kind=kLoop, calls=%fused_computation.110 | loop fusion | flops 44 | bytes 32 | tf_op jit(solution)/shard_map/reduce_sum | solution.py:287
  1.5 0.7 %fusion.44 = s32[4]{0:T(128)S(1)} fusion(s32[1,4]{1,0:T(1,128)} %param.16), kind=kLoop, calls=%fused_computation.116 | loop fusion | flops 12 | bytes 32 | tf_op jit(solution)/shard_map/select_n | solution.py:282
  2.2 1.2 %iota_compare_fusion.1 = (pred[4]{0:T(512)(128)(4,1)S(1)}, pred[4]{0:T(512)(128)(4,1)}) fusion(s32[]{:T(128)} %bitcast.57, s32[4]{0:T(128)S(1)} %select_reduce_fusion), kind=kLoop, calls=%fused_computation.119 | loop fusion | flops 8 | bytes 28 | tf_op jit(solution)/shard_map/lt | solution.py:280
  3.4 0.7 %convert_element_type.112 = f32[192]{0:T(256)S(1)} convert(bf16[192]{0:T(256)(128)(2,1)} %param.22) | non-fusion elementwise | flops 192 | bytes 1152 | tf_op jit(solution)/shard_map/convert_element_type | solution.py:27
  4.1 0.7 %convert_element_type.107 = f32[192]{0:T(256)S(1)} convert(bf16[192]{0:T(256)(128)(2,1)} %param.19) | non-fusion elementwise | flops 192 | bytes 1152 | tf_op jit(solution)/shard_map/convert_element_type | solution.py:27
  4.7 0.7 %convert_element_type.116 = f32[384]{0:T(512)S(1)} convert(bf16[384]{0:T(512)(128)(2,1)} %param.25) | non-fusion elementwise | flops 384 | bytes 2304 | tf_op jit(solution)/shard_map/convert_element_type | solution.py:27
  5.5 0.6 broadcast_in_dim.114
  6.1 0.6 pad_clamp_fusion
  6.8 1.4 %gather_fusion.2 = bf16[4,4,4,384]{3,2,1,0:T(4,128)(2,1)S(1)} fusion(bf16[4,4,4,384]{3,2,1,0:T(4,128)(2,1)} %param.15, s32[1024]{0:T(1024)S(1)} %pad_clamp_fusion.1), kind=kCustom, calls=%fused_computation.2 | custom fusion | bytes 98320 | tf_op jit(solution)/shard_map/gather | solution.py:283
  8.3 0.6 copy-done.5
  8.9 1.5 %gather_fusion = bf16[4,8,8,192]{3,2,1,0:T(8,128)(2,1)S(1)} fusion(bf16[4,8,8,192]{3,2,1,0:T(8,128)(2,1)} %param.14, s32[1024]{0:T(1024)S(1)} %pad_clamp_fusion.1), kind=kCustom, calls=%fused_computation | custom fusion | bytes 196624 | tf_op jit(solution)/shard_map/gather | solution.py:282
  10.6 2.2 %fusion.63 = (f32[4,8,8]{0,2,1:T(8,128)S(1)}, f32[4,8,8,192]{3,0,2,1:T(4,128)S(1)}) fusion(bf16[7,7,1,192]{3,1,0,2:T(8,128)(2,1)} %bitcast.60, bf16[4,8,8,192]{3,2,1,0:T(8,128)(2,1)S(1)} %broadcast_select_fusion), kind=kOutput, calls=%fused_computation.134 | convolution fusion | flops 3022592 | bytes 314752 | tf_op jit(solution)/shard_map/conv_general_dilated | solution.py:12
  12.8 0.3 multiply_reduce_fusion
  13.1 0.2 multiply_convert_fusion.2
  13.4 2.9 %multiply_convert_fusion = (bf16[256,768]{1,0:T(8,128)(2,1)S(1)}, f32[256,768]{1,0:T(8,128)}, f32[256,768]{1,0:T(8,128)}) fusion(bf16[256,192]{1,0:T(8,128)(2,1)S(1)} %bitcast.55, bf16[192,768]{1,0:T(8,128)(2,1)S(1)} %copy-done.23), kind=kOutput, calls=%fused_computation.25 | convolution fusion | flops 88276992 | bytes 2359296 | tf_op jit(solution)/shard_map/dot_general | solution.py:59
  16.2 0.3 fusion.64
  16.8 0.4 copy-done.11
  17.7 0.2 convolution_convert_fusion.7
  17.9 0.6 %fusion.65 = (f32[4,4,4]{0,2,1:T(4,128)S(1)}, f32[4,4,4,384]{3,0,2,1:T(4,128)S(1)}) fusion(bf16[7,7,1,384]{3,1,0,2:T(8,128)(2,1)S(1)} %bitcast.59, bf16[4,4,4,384]{3,2,1,0:T(4,128)(2,1)S(1)} %reshape.188), kind=kOutput, calls=%fused_computation.136 | convolution fusion | flops 810944 | bytes 185344 | tf_op jit(solution)/shard_map/conv_general_dilated | solution.py:12
  18.6 0.2 multiply_reduce_fusion.4
  18.8 0.6 copy-done.9
  19.6 0.2 copy.99
  19.8 0.3 fusion.66
  20.1 0.4 copy-done.4
  20.5 0.5 copy-done.22
  21.0 1.6 %fusion.6 = bf16[64,384]{1,0:T(8,128)(2,1)} fusion(bf16[1536,384]{1,0:T(8,128)(2,1)S(1)} %copy-done.22, f32[64,1536]{1,0:T(8,128)S(1)} %fusion.66, bf16[64,384]{1,0:T(8,128)(2,1)S(1)} %copy-done.4), kind=kOutput, calls=%fused_computation.19 | convolution fusion | flops 81960960 | bytes 1671168 | tf_op jit(solution)/shard_map/dot_general | solution.py:83
  22.7 3.3 %fusion.7 = f32[64,384]{1,0:T(8,128)} fusion(bf16[384,1536]{1,0:T(8,128)(2,1)S(1)} %copy-done, bf16[1536,384]{1,0:T(8,128)(2,1)} %param.27, f32[64,1536]{1,0:T(8,128)S(1)} %fusion.66, bf16[64,384]{1,0:T(8,128)(2,1)S(1)} %gather.17, pred[64]{0:T(512)(128)(4,1)S(1)} %copy-done.20), kind=kOutput, calls=%fused_computation.21 | convolution fusion | flops 158343168 | bytes 2900032 | tf_op jit(solution)/shard_map/dot_general | solution.py:91
  25.9 0.9 %reshape.196 = f32[4,4,4,384]{3,2,1,0:T(4,128)S(1)} reshape(f32[64,384]{1,0:T(8,128)} %fusion.7) | data formatting | bytes 196608 | tf_op jit(solution)/shard_map/reshape | solution.py:96
  26.8 0.8 %reshape.190 = bf16[4,4,4,384]{3,2,1,0:T(4,128)(2,1)S(1)} reshape(bf16[64,384]{1,0:T(8,128)(2,1)} %fusion.6) | data formatting | bytes 98304 | tf_op jit(solution)/shard_map/reshape | solution.py:122
  27.6 0.7 %gather_fusion.1 = bf16[4,4,4,384]{3,2,1,0:T(4,128)(2,1)S(1)} fusion(bf16[4,4,4,384]{3,2,1,0:T(4,128)(2,1)S(1)} %reshape.190, s32[1024]{0:T(1024)} %pad_clamp_fusion), kind=kCustom, calls=%fused_computation.1 | custom fusion | bytes 98320 | tf_op jit(solution)/shard_map/gather | solution.py:290
  28.4 0.8 %copy_select_fusion.1 = bf16[4,4,4,384]{3,0,2,1:T(4,128)(2,1)S(1)} fusion(bf16[4,4,4,384]{3,2,1,0:T(4,128)(2,1)S(1)} %gather_fusion.1, pred[4]{0:T(512)(128)(4,1)} %get-tuple-element.38), kind=kLoop, calls=%fused_computation.95 | loop fusion | flops 24576 | bytes 98308 | tf_op jit(solution)/shard_map/jit(_where)/select_n | solution.py:290
  29.1 0.6 copy.95
  29.8 0.9 %multiply_reduce_fusion.3 = f32[4,4,4]{0,2,1:T(4,128)S(1)} fusion(f32[4,4,4,384]{3,2,1,0:T(4,128)S(1)} %reshape.196, f32[4,4,4,384]{3,0,2,1:T(4,128)S(1)} %get-tuple-element.34, f32[384]{0:T(512)} %copy-done.10, f32[4,4,4]{0,2,1:T(4,128)S(1)} %broadcast_multiply_fusion.1), kind=kLoop, calls=%fused_computation.87 | loop fusion | flops 98240 | bytes 198656 | tf_op jit(solution)/shard_map/transpose(jvp())/reduce_sum | solution.py:27
  30.7 0.9 %fusion.56 = f32[4,4,4]{0,2,1:T(4,128)S(1)} fusion(f32[4,4,4]{0,2,1:T(4,128)S(1)} %multiply_multiply_fusion.10, f32[4,4,4,384]{3,0,2,1:T(4,128)S(1)} %get-tuple-element.34, f32[4,4,4]{0,2,1:T(4,128)S(1)} %broadcast_multiply_fusion.1, f32[4,4,4]{0,2,1:T(4,128)} %copy-done.9, f32[384]{0:T(512)} %copy-done.10, f32[4,4,4,384]{3,2,1,0:T(4,128)S(1)} %reshape.196), kind=kLoop, calls=%fused_computation.130 | loop fusion | flops 171968 | bytes 199168 | tf_op jit(solution)/shard_map/transpose(jvp())/reduce_sum | solution.py:25
  31.6 1.4 %add_convert_fusion.4 = (bf16[4,4,4,384]{3,0,2,1:T(4,128)(2,1)S(1)}, f32[4,4,4,384]{3,0,2,1:T(4,128)S(1)}) fusion(bf16[4,4,4,384]{3,2,1,0:T(4,128)(2,1)S(1)} %copy-done.6, pred[4]{0:T(512)(128)(4,1)} %copy-done.19, bf16[7,7,384,1]{2,1,0,3:T(8,128)(2,1)} %bitcast.58, f32[4,4,4]{0,2,1:T(4,128)S(1)} %negate_multiply_fusion.4, ...), kind=kOutput, calls=%fused_computation.84 | convolution fusion | flops 4988928 | bytes 433412 | tf_op jit(solution)/shard_map/transpose(jvp())/conv_general_dilated | solution.py:12
  33.2 0.3 fusion.5
  33.6 0.2 reshape.198
  33.9 0.2 reshape.197
  34.5 0.2 copy-done.8
  34.7 2.0 %convolution_convert_fusion.4 = bf16[768,192]{0,1:T(8,128)(2,1)S(1)} fusion(bf16[256,192]{1,0:T(8,128)(2,1)S(1)} %bitcast.56, f32[256,768]{1,0:T(8,128)} %get-tuple-element.23, bf16[768,192]{0,1:T(8,128)(2,1)S(1)} %copy-done.2, f32[256,768]{1,0:T(8,128)} %get-tuple-element.30, f32[256,192]{0,1:T(8,128)S(1)} %get-tuple-element.21, ...), kind=kOutput, calls=%fused_computation.10 | convolution fusion | flops 154386432 | bytes 2458624 | tf_op jit(solution)/shard_map/dot_general | solution.py:120
  36.7 0.2 convolution_convert_fusion.3
  37.0 0.3 copy.93
  37.3 0.3 fusion.1
  37.6 0.1 maximum_bitcast_fusion.halves
  37.8 24.1 %shard_map.165 = f32[2,2,48,384]{3,2,1,0:T(8,128)S(1)} custom-call(bf16[2,4,4,48,384]{4,3,2,1,0:T(8,128)(2,1)S(1)} %maximum_bitcast_fusion.halves), custom_call_target="tpu_custom_call" | custom-call | flops 1000000 | bytes 4000000 | tf_op jit(solution)/shard_map/pallas_call | solution.py:204
  61.9 0.7 %fusion.61 = (f32[1,2,48,384]{3,2,1,0:T(8,128)}, f32[1,2,48,384]{3,2,1,0:T(8,128)S(1)}) fusion(f32[2,2,48,384]{3,2,1,0:T(8,128)S(1)} %shard_map.165), kind=kLoop, calls=%fused_computation.132 | loop fusion | bytes 589824 | tf_op jit(solution)/shard_map/slice | solution.py:237
  62.6 0.7 %fusion.62 = (f32[96,192]{1,0:T(8,128)}, f32[192,96]{0,1:T(8,128)S(1)}) fusion(f32[96,384]{1,0:T(8,128)S(1)} %bitcast.51), kind=kLoop, calls=%fused_computation.133 | loop fusion | bytes 294912 | tf_op jit(solution)/shard_map/slice | solution.py:241
  63.3 0.7 %copy.96 = f32[192,96]{1,0:T(8,128)} copy(f32[192,96]{0,1:T(8,128)S(1)} %get-tuple-element.27) | data formatting | bytes 147456
  (82 shorter events, 2.0 us)
Async XLA Ops:
  0.6 19.1 %copy-start = (bf16[384,1536]{1,0:T(8,128)(2,1)S(1)}, bf16[384,1536]{1,0:T(8,128)(2,1)}, u32[]{:S(2)}) copy-start(bf16[384,1536]{1,0:T(8,128)(2,1)} %param.26) | copy-start | bytes 3538948
  3.4 7.1 %copy-start.19 = (pred[4]{0:T(512)(128)(4,1)}, pred[4]{0:T(512)(128)(4,1)S(1)}, u32[]{:S(2)}) copy-start(pred[4]{0:T(512)(128)(4,1)S(1)} %get-tuple-element.37) | copy-start | bytes 16
  4.1 12.6 %copy-start.13 = (f32[192]{0:T(256)}, f32[192]{0:T(256)S(1)}, u32[]{:S(2)}) copy-start(f32[192]{0:T(256)S(1)} %convert_element_type.112) | copy-start | bytes 2308
  5.4 13.4 %copy-start.10 = (f32[384]{0:T(512)}, f32[384]{0:T(512)S(1)}, u32[]{:S(2)}) copy-start(f32[384]{0:T(512)S(1)} %convert_element_type.116) | copy-start | bytes 4612
  8.2 0.6 copy-start.5
  10.4 3.0 %copy-start.23 = (bf16[192,768]{1,0:T(8,128)(2,1)S(1)}, bf16[192,768]{1,0:T(8,128)(2,1)}, u32[]{:S(2)}) copy-start(bf16[192,768]{1,0:T(8,128)(2,1)} %param.20) | copy-start | bytes 884740
  13.3 2.9 %copy-start.7 = (bf16[4,8,8,192]{3,2,1,0:T(8,128)(2,1)}, bf16[4,8,8,192]{3,2,1,0:T(8,128)(2,1)S(1)}, u32[]{:S(2)}) copy-start(bf16[4,8,8,192]{3,2,1,0:T(8,128)(2,1)S(1)} %copy.77) | copy-start | bytes 294916
  13.3 2.9 %copy-start.2 = (bf16[768,192]{0,1:T(8,128)(2,1)S(1)}, bf16[768,192]{0,1:T(8,128)(2,1)}, u32[]{:S(2)}) copy-start(bf16[768,192]{0,1:T(8,128)(2,1)} %param.21) | copy-start | bytes 884740
  16.2 1.4 %copy-start.1 = (bf16[768,384]{1,0:T(8,128)(2,1)S(1)}, bf16[768,384]{1,0:T(8,128)(2,1)}, u32[]{:S(2)}) copy-start(bf16[768,384]{1,0:T(8,128)(2,1)} %param.23) | copy-start | bytes 1769476
  16.5 1.4 %copy-start.24 = (bf16[7,7,384]{2,1,0:T(8,128)(2,1)S(1)}, bf16[7,7,384]{2,1,0:T(8,128)(2,1)}, u32[]{:S(2)}) copy-start(bf16[7,7,384]{2,1,0:T(8,128)(2,1)} %param.24) | copy-start | bytes 112900
  16.6 0.6 copy-start.11
  16.6 0.6 copy-start.17
  16.7 0.6 copy-start.15
  17.9 1.6 %copy-start.3 = (bf16[64,384]{1,0:T(8,128)(2,1)}, bf16[64,384]{1,0:T(8,128)(2,1)S(1)}, u32[]{:S(2)}) copy-start(bf16[64,384]{1,0:T(8,128)(2,1)S(1)} %convolution_convert_fusion.7) | copy-start | bytes 147460
  18.8 0.6 copy-start.9
  19.7 0.8 %copy-start.4 = (bf16[64,384]{1,0:T(8,128)(2,1)S(1)}, bf16[64,384]{1,0:T(8,128)(2,1)}, u32[]{:S(2)}) copy-start(bf16[64,384]{1,0:T(8,128)(2,1)} %copy-done.3) | copy-start | bytes 147460
  19.7 1.3 %copy-start.22 = (bf16[1536,384]{1,0:T(8,128)(2,1)S(1)}, bf16[1536,384]{1,0:T(8,128)(2,1)}, u32[]{:S(2)}) copy-start(bf16[1536,384]{1,0:T(8,128)(2,1)} %param.27) | copy-start | bytes 3538948
  21.0 1.6 %copy-start.20 = (pred[64]{0:T(512)(128)(4,1)S(1)}, pred[64]{0:T(512)(128)(4,1)}, u32[]{:S(2)}) copy-start(pred[64]{0:T(512)(128)(4,1)} %broadcast_in_dim.114) | copy-start | bytes 196
  22.7 8.9 %copy-start.6 = (bf16[4,4,4,384]{3,2,1,0:T(4,128)(2,1)S(1)}, bf16[4,4,4,384]{3,2,1,0:T(4,128)(2,1)}, u32[]{:S(2)}) copy-start(bf16[4,4,4,384]{3,2,1,0:T(4,128)(2,1)} %copy-done.5) | copy-start | bytes 147460
  29.1 4.0 %copy-start.21 = (pred[64]{0:T(512)(128)(4,1)S(1)}, pred[64]{0:T(512)(128)(4,1)}, u32[]{:S(2)}) copy-start(pred[64]{0:T(512)(128)(4,1)} %broadcast_in_dim.114) | copy-start | bytes 196
  33.5 0.7 %copy-start.12 = (f32[256]{0:T(256)S(1)}, f32[256]{0:T(256)}, u32[]{:S(2)}) copy-start(f32[256]{0:T(256)} %copy-done.11) | copy-start | bytes 3076
  33.5 0.7 %copy-start.14 = (f32[192]{0:T(256)S(1)}, f32[192]{0:T(256)}, u32[]{:S(2)}) copy-start(f32[192]{0:T(256)} %copy-done.13) | copy-start | bytes 2308
  33.5 0.8 %copy-start.18 = (f32[256]{0:T(256)S(1)}, f32[256]{0:T(256)}, u32[]{:S(2)}) copy-start(f32[256]{0:T(256)} %copy-done.17) | copy-start | bytes 3076
  33.5 0.8 %copy-start.16 = (f32[256]{0:T(256)S(1)}, f32[256]{0:T(256)}, u32[]{:S(2)}) copy-start(f32[256]{0:T(256)} %copy-done.15) | copy-start | bytes 3076
  33.8 0.9 %copy-start.8 = (bf16[4,8,8,192]{3,2,1,0:T(8,128)(2,1)S(1)}, bf16[4,8,8,192]{3,2,1,0:T(8,128)(2,1)}, u32[]{:S(2)}) copy-start(bf16[4,8,8,192]{3,2,1,0:T(8,128)(2,1)} %copy-done.7) | copy-start | bytes 294916

commit v2 on v1

v2 whole, which is shorter than its diff:
```python
import functools

import jax
import jax.numpy as jnp
from jax import lax
from jax.experimental import pallas as pl
from jax.experimental.pallas import tpu as pltpu
from jax.sharding import PartitionSpec as P

MESH = pl.DeviceIdType.MESH


def exchange_kernel(line, halves, out, get_pair, put_quad, get_quad, mine, put_line, get_line, put_rep, get_rep, pair_sems, quad_sems, line_sems, rep_sems):
    s = lax.axis_index("slide")
    r = lax.axis_index("rep")
    core, y = r % 2, r // 2
    x, z = s % 2, s // 2
    spot = x * 2 + y
    pair_peer = (s, y * 2 + 1 - core)

    def quad_peer(d):
        return (z * 2 + (x + d // 2) % 2, ((y + d) % 2) * 2 + core)

    def line_peer(d):
        return (((z + d) % line) * 2 + x, r)

    def rep_peer(d):
        return (s, ((y + d // 2) % 2) * 2 + (core + d) % 2)

    def quad_spot(d):
        return ((x + d // 2) % 2) * 2 + (y + d) % 2

    barrier = pltpu.get_barrier_semaphore()
    peers = [rep_peer(d) for d in (1, 2, 3)] + [quad_peer(d) for d in (2, 3)] + [line_peer(d) for d in range(1, line)]
    for peer in peers:
        pl.semaphore_signal(barrier, inc=1, device_id=peer, device_id_type=MESH)
    pl.semaphore_wait(barrier, len(peers))

    def send(src, dst, sems, slot, peer):
        copy = pltpu.make_async_remote_copy(
            src_ref=src, dst_ref=dst, send_sem=sems.at[0, slot], recv_sem=sems.at[1, slot],
            device_id=peer, device_id_type=MESH)
        copy.start()
        return copy

    pairs = {}
    for d in (3, 2, 1, 0):
        pairs[d] = send(halves.at[1 - core, quad_spot(d)], get_pair.at[d], pair_sems, d, pair_peer)
    quads = {}
    for d in (3, 2, 1):
        pairs[d].wait_recv()
        put_quad[d - 1] = (halves[core, quad_spot(d)].astype(jnp.float32) + get_pair[d].astype(jnp.float32)).astype(jnp.bfloat16)
        quads[d] = send(put_quad.at[d - 1], get_quad.at[d - 1], quad_sems, d - 1, quad_peer(d))
    pairs[0].wait_recv()
    mine[...] = halves[core, spot].astype(jnp.float32) + get_pair[0].astype(jnp.float32)
    for d in (1, 2, 3):
        quads[d].wait_recv()
    lines = {}
    for d in [*range(line - 1, 0, -1), 0]:
        at = (z + d) % line
        part = mine[at] + get_quad[0, at].astype(jnp.float32) + get_quad[1, at].astype(jnp.float32) + get_quad[2, at].astype(jnp.float32)
        if d:
            put_line[d - 1] = part.astype(jnp.bfloat16)
            lines[d] = send(put_line.at[d - 1], get_line.at[d - 1], line_sems, d - 1, line_peer(d))
        else:
            total = part
    for d in range(1, line):
        lines[d].wait_recv()
        total = total + get_line[d - 1].astype(jnp.float32)
    put_rep[...] = total.astype(jnp.bfloat16)
    reps = {}
    for d in (3, 2, 1):
        reps[d] = send(put_rep, get_rep.at[d - 1], rep_sems, d - 1, rep_peer(d))
    out[core, y] = put_rep[...].astype(jnp.float32)
    for d in (1, 3, 2):
        reps[d].wait_recv()
        out[(core + d) % 2, (y + d // 2) % 2] = get_rep[d - 1].astype(jnp.float32)
    for copy in [*pairs.values(), *quads.values(), *lines.values(), *reps.values()]:
        copy.wait_send()


def exchange(halves, slides):
    line = slides // 2
    block = halves.shape[-2:]
    return pl.pallas_call(
        functools.partial(exchange_kernel, line),
        out_shape=jax.ShapeDtypeStruct((2, 2) + block, jnp.float32),
        in_specs=[pl.BlockSpec(memory_space=pltpu.VMEM)],
        out_specs=pl.BlockSpec(memory_space=pltpu.VMEM),
        scratch_shapes=[
            pltpu.VMEM((4, line) + block, jnp.bfloat16),
            pltpu.VMEM((3, line) + block, jnp.bfloat16),
            pltpu.VMEM((3, line) + block, jnp.bfloat16),
            pltpu.VMEM((line,) + block, jnp.float32),
            pltpu.VMEM((line - 1,) + block, jnp.bfloat16),
            pltpu.VMEM((line - 1,) + block, jnp.bfloat16),
            pltpu.VMEM(block, jnp.bfloat16),
            pltpu.VMEM((3,) + block, jnp.bfloat16),
            pltpu.SemaphoreType.DMA((2, 4)),
            pltpu.SemaphoreType.DMA((2, 3)),
            pltpu.SemaphoreType.DMA((2, line - 1)),
            pltpu.SemaphoreType.DMA((2, 3)),
        ],
        compiler_params=pltpu.CompilerParams(collective_id=0, has_side_effects=True, vmem_limit_bytes=48 * 1024 * 1024),
        cost_estimate=pl.CostEstimate(flops=10**6, bytes_accessed=4 * 10**6, transcendentals=0),
    )(halves)


def dot(a, b, contract=(1, 0)):
    return lax.dot_general(a, b, (((contract[0],), (contract[1],)), ((), ())), preferred_element_type=jnp.float32)


def centre_scale(values):
    offset = values - jnp.mean(values, axis=-1, keepdims=True)
    scale = lax.rsqrt(jnp.mean(offset * offset, axis=-1, keepdims=True) + 1e-06)
    return offset * scale, scale


def norm_back(grad, unit, scale):
    return scale * (grad - jnp.mean(grad, axis=-1, keepdims=True) - unit * jnp.mean(grad * unit, axis=-1, keepdims=True))


def gelu_rows(expand, hidden, slope, rows, columns):
    across = expand.shape[1] // columns

    def body(i, carry):
        here = pl.ds(pl.multiple_of(i * rows, rows), rows)
        for c in range(across):
            there = slice(c * columns, (c + 1) * columns)
            v = expand[here, there]
            below = 0.5 + 0.5 * lax.erf(v * 0.7071067811865476)
            hidden[here, there] = (v * below).astype(jnp.bfloat16)
            slope[here, there] = below + v * (jnp.exp(v * v * -0.5) * 0.3989422804014327)
        return carry

    lax.fori_loop(0, expand.shape[0] // rows, body, 0)


def side_sum(shifted, taps, out, flip):
    span, side = shifted.shape[0], shifted.shape[1]
    reach = span // 2
    for i in range(side):
        total = None
        for other in range(max(0, i - reach), min(side, i + reach + 1)):
            row = reach + (i - other if flip else other - i)
            for d in range(span):
                term = shifted[d, other] * taps[row, (span - 1 - d) if flip else d]
                total = term if total is None else total + term
        out[i] = total


def compute_kernel(feats, cot, keep, plan, kernel_one, gain_one, inward_one, outward_one, gain_down, project, kernel_two,
                   gain_two, inward_two, outward_two, features, halves, pad_one, shift_one, taps_one, conv_one, expand, hidden,
                   slope, pad_two, shift_two, taps_two, conv_two, rows_two, expand_two, hidden_two, slope_two):
    tiles, side, _, narrow = feats.shape
    half = side // 2
    wide = project.shape[1]
    span = kernel_one.shape[0]
    reach = span // 2
    rows, small = tiles * side * side, tiles * half * half
    f32, bf16 = jnp.float32, jnp.bfloat16
    lives = []
    for t in range(tiles):
        place = sum(jnp.where(keep[0, p] == t, p, 0) for p in range(tiles))
        lives.append(jnp.where(place < plan[0, 0], 1.0, 0.0).astype(f32))

    for d in range(span):
        taps_one[d] = jnp.broadcast_to(kernel_one[d].astype(f32)[:, None, :], (span, 8, narrow))
        taps_two[d] = jnp.broadcast_to(kernel_two[d].astype(f32)[:, None, :], (span, 8, wide))
    pad_one[...] = jnp.zeros_like(pad_one)
    for t in range(tiles):
        pad_one[:, t, 8:8 + side, :] = feats[t].astype(f32) * lives[t]
    for d in range(span):
        shift_one[d] = pad_one[:, :, 8 + d - reach:8 + d - reach + side, :]
    side_sum(shift_one, taps_one, conv_one, False)
    unit, _ = centre_scale(conv_one[...].reshape(rows, narrow))
    normed = (unit * gain_one[...].astype(f32)).astype(bf16)
    plain = pad_one[:, :, 8:8 + side, :].reshape(rows, narrow).astype(bf16)
    to = lax.broadcasted_iota(jnp.int32, (rows, rows), 0)
    column_pair, rest = to & (half - 1), to >> (half.bit_length() - 1)
    tile, rest = rest & (tiles - 1), rest >> (tiles.bit_length() - 1)
    row_pair, rest = rest & (half - 1), rest >> (half.bit_length() - 1)
    source = ((row_pair * 2 + (rest >> 1)) * tiles + tile) * side + column_pair * 2 + (rest & 1)
    order = jnp.where(lax.broadcasted_iota(jnp.int32, (rows, rows), 1) == source, 1.0, 0.0).astype(bf16)
    normed = dot(order, normed).astype(bf16)
    plain = dot(order, plain)
    expand[...] = dot(normed, inward_one[...])
    gelu_rows(expand, hidden, slope, 16, expand.shape[1])
    section = (plain + dot(hidden[...], outward_one[...])).astype(bf16).astype(f32)
    unit_down, scale_down = centre_scale(section)
    gain = gain_down[...].astype(f32)
    down = (unit_down * gain).astype(bf16)
    merged = sum(dot(down[q * small:(q + 1) * small], project[q * narrow:(q + 1) * narrow]) for q in range(4)).astype(bf16).astype(f32)

    lane = lax.broadcasted_iota(jnp.int32, (half, tiles * half, wide), 1) & (half - 1)

    def second_conv(values, flip):
        pad_two[...] = jnp.zeros_like(pad_two)
        pad_two[:, 8:8 + tiles * half, :] = values.reshape(half, tiles * half, wide)
        for d in range(span):
            at = lane + (d - reach)
            moved = pad_two[:, 8 + d - reach:8 + d - reach + tiles * half, :]
            shift_two[d] = jnp.where((at >= 0) & (at < half), moved, 0.0).reshape(half, tiles * half // 8, 8, wide)
        side_sum(shift_two, taps_two, conv_two, flip)
        return conv_two[...].reshape(small, wide)

    unit_two, scale_two = centre_scale(second_conv(merged, False))
    second_gain = gain_two[...].astype(f32)
    normed_two = (unit_two * second_gain).astype(bf16)
    expand_two[...] = dot(normed_two, inward_two[...])
    gelu_rows(expand_two, hidden_two, slope_two, 16, expand_two.shape[1] // 2)
    rows_two[...] = merged + dot(hidden_two[...], outward_two[...])
    for t in range(tiles):
        for i in range(half):
            at = (i * tiles + t) * half
            features[t, i] = (rows_two[at:at + half] * lives[t]).astype(bf16)
    for t in range(tiles):
        for i in range(half):
            at = (i * tiles + t) * half
            rows_two[at:at + half] = cot[t, i].astype(f32) * lives[t]
    cotangent = rows_two[...]
    back = dot(cotangent.astype(bf16), outward_two[...], (1, 1)).astype(bf16).astype(f32)
    back = (slope_two[...] * back).astype(bf16)
    back = dot(back, inward_two[...], (1, 1)).astype(bf16).astype(f32)
    back = second_conv(norm_back(back * second_gain, unit_two, scale_two), True)
    back_merged = (cotangent + back).astype(bf16)

    spots, line, part = halves.shape[1:4]

    def put(where, start, value):
        for at in range(0, value.shape[0], part):
            whole = (start + at) // part
            halves[where, whole % spots, whole // spots] = value[at:at + part].astype(halves.dtype)

    grad_project = jnp.concatenate([dot(down[q * small:(q + 1) * small], back_merged, (0, 0)) for q in range(4)], axis=0)
    put(0, 0, grad_project)
    back_down = jnp.concatenate([dot(back_merged, project[q * narrow:(q + 1) * narrow], (1, 1)) for q in range(4)], axis=0)
    back_down = back_down.astype(bf16).astype(f32)
    back_section = norm_back(back_down * gain, unit_down, scale_down).astype(bf16)
    grad_outward = dot(hidden[...], back_section, (0, 0))
    back_hidden = dot(back_section, outward_one[...], (1, 1)).astype(bf16).astype(f32)
    back_expand = (slope[...] * back_hidden).astype(bf16)
    grad_inward = dot(back_expand, normed, (0, 0))
    put(1, 0, jnp.concatenate([grad_inward, grad_outward], axis=1))


def compute_scratch(tiles, side, narrow, wide, span, inner, inner_two):
    half = side // 2
    rows, small = tiles * side * side, tiles * half * half
    f32, bf16 = jnp.float32, jnp.bfloat16
    return [
        pltpu.VMEM((side, tiles, side + 16, narrow), f32),
        pltpu.VMEM((span, side, tiles, side, narrow), f32),
        pltpu.VMEM((span, span, 8, narrow), f32),
        pltpu.VMEM((side, tiles, side, narrow), f32),
        pltpu.VMEM((rows, inner), f32),
        pltpu.VMEM((rows, inner), bf16),
        pltpu.VMEM((rows, inner), f32),
        pltpu.VMEM((half, tiles * half + 16, wide), f32),
        pltpu.VMEM((span, half, tiles * half // 8, 8, wide), f32),
        pltpu.VMEM((span, span, 8, wide), f32),
        pltpu.VMEM((half, tiles * half // 8, 8, wide), f32),
        pltpu.VMEM((small, wide), f32),
        pltpu.VMEM((small, inner_two), f32),
        pltpu.VMEM((small, inner_two), bf16),
        pltpu.VMEM((small, inner_two), f32),
    ]


def fits(slides, reps, rows):
    return reps == 4 and slides % 2 == 0 and slides > 2 and rows % (slides * 32) == 0


def per_device(tile_feats, cotangent, keep_list, tile_plan, kernel_one, gain_one, inward_one, outward_one, gain_down,
               project_down, kernel_two, gain_two, inward_two, outward_two):
    slides, reps = lax.axis_size("slide"), lax.axis_size("rep")
    rows, wide = project_down.shape
    narrow = tile_feats.shape[3]
    direct = fits(slides, reps, rows)
    cut = (4, slides // 2, rows // slides // 2) if direct else (1, 1, rows)
    whole = pl.BlockSpec(memory_space=pltpu.VMEM)
    scalars = pl.BlockSpec(memory_space=pltpu.SMEM)
    features, halves = pl.pallas_call(
        compute_kernel,
        out_shape=(
            jax.ShapeDtypeStruct(cotangent.shape, jnp.bfloat16),
            jax.ShapeDtypeStruct((2,) + cut + (wide,), jnp.bfloat16 if direct else jnp.float32),
        ),
        in_specs=[whole, whole, scalars, scalars] + [whole] * 10,
        out_specs=(whole, whole),
        scratch_shapes=compute_scratch(
            tile_feats.shape[0], tile_feats.shape[1], narrow, wide, kernel_one.shape[0], inward_one.shape[1], inward_two.shape[1]),
        compiler_params=pltpu.CompilerParams(vmem_limit_bytes=48 * 1024 * 1024),
    )(tile_feats, cotangent, keep_list, tile_plan, kernel_one, gain_one[None], inward_one, outward_one, gain_down[None],
      project_down, kernel_two, gain_two[None], inward_two, outward_two)
    if direct:
        got = exchange(halves, slides).reshape(2, rows // slides, wide)
        project, both = got[0], got[1]
    else:
        project, both = (
            lax.psum(lax.psum_scatter(g.reshape(rows, wide), "slide", scatter_dimension=0, tiled=True), "rep")
            for g in (halves[0], halves[1]))
    return features, both[:, :narrow].T, both[:, narrow:], project


def solution(mesh):
    in_specs = (
        P(("slide", "rep"), None, None, None),
        P(("slide", "rep"), None, None, None),
        P(("slide", "rep"), None),
        P(("slide", "rep"), None),
        P(),
        P(),
        P(),
        P(),
        P(),
        P(),
        P(),
        P(),
        P(),
        P(),
    )
    out_specs = (
        P(("slide", "rep"), None, None, None),
        P(None, "slide"),
        P("slide", None),
        P("slide", None),
    )
    return jax.shard_map(
        per_device, mesh=mesh, in_specs=in_specs, out_specs=out_specs, check_vma=False
    )
```

time: 64.7 us -> 47.4 us (0.73)
  matrix products: 15.7 us -> 0 us
  other arithmetic: 9.34 us -> 0 us
  Pallas kernels: 24.1 us -> 31.8 us
  local copies, waits for them, and re-layouts: 13.6 us -> 14.4 us
    dot_general x10 -> x0, matrix products: 11.4 us -> none  [the longest x1 3.25 us: slot_pass(): jnp.dot(back_expand_two, inward_two.T, preferred_element_type=jnp.float32)]
    pallas_call x0 -> x1, Pallas kernels: none -> 7.7 us  [per_device(): pl.pallas_call(compute_kernel, out_shape=(jax.ShapeDtypeStruct(cotangent....]
    unnamed x52 -> x22, local copies, waits for them, and re-layouts: 4.35 us -> 11 us
    conv_general_dilated x3 -> x0, matrix products: 4.3 us -> none  [depthwise(): lax.conv_general_dilated(field.astype(jnp.float32), kernel.astype(jnp.flo...]
    gather x5 -> x0, local copies, waits for them, and re-layouts: 3.7 us -> none  [the longest x2 1.56 us: per_device(): tile_feats[ordering]]
    reduce_sum x8 -> x0, other arithmetic: 3.35 us -> none  [the longest x2 1.03 us: layer_norm(): offset = values - centre]
    convert_element_type x6 -> x0, other arithmetic: 2.4 us -> none  [the longest x3 2 us: layer_norm(): return offset * lax.rsqrt(spread + 1e-06) * gain.astype(jnp.float32)]
    reshape x7 -> x0, local copies, waits for them, and re-layouts: 2.02 us -> none  [the longest x1 0.92 us: slot_pass(): back_normed_two.astype(jnp.float32)]
where the time goes in v2:
time: 47.4 us; the launch traced here: 46.9 us
  Pallas kernels  31.8 us (67%)
  local copies, waits for them, and re-layouts  14.4 us (30%)
  between operations  0.67 us (1%)
    pallas_call x1, Pallas kernels, exchange(): pl.pallas_call(functools.partial(exchange_kernel, line), out_shape=jax.Sh...  24.1 us
    unnamed x22, local copies, waits for them, and re-layouts  11 us
    pallas_call x1, Pallas kernels, per_device(): pl.pallas_call(compute_kernel, out_shape=(jax.ShapeDtypeStruct(cotangent....  7.7 us

profile of v2, /device:TPU:0, one launch (start us, length us, event | category | flops | bytes accessed | tf_op | source)
XLA Modules:
  0.0 46.9 jit_solution(14763323390473569282)
XLA Ops:
  0.6 0.7 %broadcast_in_dim.9.gain_one = bf16[1,192]{1,0:T(2,128)(2,1)S(1)} reshape(bf16[192]{0:T(256)(128)(2,1)} %param.19) | data formatting | bytes 768 | tf_op jit(solution)/shard_map/broadcast_in_dim | solution.py:294
  1.3 0.7 %broadcast_in_dim.10.gain_down = bf16[1,192]{1,0:T(2,128)(2,1)S(1)} reshape(bf16[192]{0:T(256)(128)(2,1)} %param.22) | data formatting | bytes 768 | tf_op jit(solution)/shard_map/broadcast_in_dim | solution.py:294
  1.9 0.7 %broadcast_in_dim.11.gain_two = bf16[1,384]{1,0:T(2,128)(2,1)S(1)} reshape(bf16[384]{0:T(512)(128)(2,1)} %param.25) | data formatting | bytes 1536 | tf_op jit(solution)/shard_map/broadcast_in_dim | solution.py:295
  2.6 1.1 %copy.18.outward_one = bf16[768,192]{1,0:T(8,128)(2,1)S(1)} copy(bf16[768,192]{0,1:T(8,128)(2,1)} %param.21) | data formatting | bytes 589824 | tf_op args[7]
  3.8 0.0 copy-start
  3.8 1.3 %copy-done = bf16[384,1536]{1,0:T(8,128)(2,1)S(1)} copy-done((bf16[384,1536]{1,0:T(8,128)(2,1)S(1)}, bf16[384,1536]{1,0:T(8,128)(2,1)}, u32[]{:S(2)}) %copy-start) | copy-done | bytes 1179672
  5.0 0.0 copy-start.1
  5.0 1.3 %copy-done.1 = bf16[1536,384]{1,0:T(8,128)(2,1)S(1)} copy-done((bf16[1536,384]{1,0:T(8,128)(2,1)S(1)}, bf16[1536,384]{1,0:T(8,128)(2,1)}, u32[]{:S(2)}) %copy-start.1) | copy-done | bytes 1179672
  6.3 0.0 copy-start.2
  6.3 1.1 %copy-done.2 = bf16[768,384]{1,0:T(8,128)(2,1)S(1)} copy-done((bf16[768,384]{1,0:T(8,128)(2,1)S(1)}, bf16[768,384]{1,0:T(8,128)(2,1)}, u32[]{:S(2)}) %copy-start.2) | copy-done | bytes 589848
  7.4 0.0 copy-start.3
  7.4 1.0 %copy-done.3 = bf16[192,768]{1,0:T(8,128)(2,1)S(1)} copy-done((bf16[192,768]{1,0:T(8,128)(2,1)S(1)}, bf16[192,768]{1,0:T(8,128)(2,1)}, u32[]{:S(2)}) %copy-start.3) | copy-done | bytes 294936
  8.3 0.0 copy-start.4
  8.3 0.9 %copy-done.4 = bf16[4,8,8,192]{3,2,1,0:T(8,128)(2,1)S(1)} copy-done((bf16[4,8,8,192]{3,2,1,0:T(8,128)(2,1)S(1)}, bf16[4,8,8,192]{3,2,1,0:T(8,128)(2,1)}, u32[]{:S(2)}) %copy-start.4) | copy-done | bytes 98328
  9.2 0.0 copy-start.5
  9.2 0.8 %copy-done.5 = bf16[4,4,4,384]{3,2,1,0:T(4,128)(2,1)S(1)} copy-done((bf16[4,4,4,384]{3,2,1,0:T(4,128)(2,1)S(1)}, bf16[4,4,4,384]{3,2,1,0:T(4,128)(2,1)}, u32[]{:S(2)}) %copy-start.5) | copy-done | bytes 49176
  10.0 0.0 copy-start.6
  10.0 0.8 %copy-done.6 = bf16[7,7,384]{2,1,0:T(8,128)(2,1)S(1)} copy-done((bf16[7,7,384]{2,1,0:T(8,128)(2,1)S(1)}, bf16[7,7,384]{2,1,0:T(8,128)(2,1)}, u32[]{:S(2)}) %copy-start.6) | copy-done | bytes 37656
  10.8 0.0 copy-start.7
  10.8 0.7 %copy-done.7 = bf16[7,7,192]{2,1,0:T(8,128)(2,1)S(1)} copy-done((bf16[7,7,192]{2,1,0:T(8,128)(2,1)S(1)}, bf16[7,7,192]{2,1,0:T(8,128)(2,1)}, u32[]{:S(2)}) %copy-start.7) | copy-done | bytes 18840
  11.6 0.0 copy-start.8
  11.6 0.7 %copy-done.8 = s32[1,4]{1,0:T(1,128)S(1)} copy-done((s32[1,4]{1,0:T(1,128)S(1)}, s32[1,4]{1,0:T(1,128)}, u32[]{:S(2)}) %copy-start.8) | copy-done | bytes 40
  12.2 0.0 copy-start.9
  12.2 0.7 %copy-done.9 = s32[1,2]{1,0:T(1,128)S(1)} copy-done((s32[1,2]{1,0:T(1,128)S(1)}, s32[1,2]{1,0:T(1,128)}, u32[]{:S(2)}) %copy-start.9) | copy-done | bytes 32
  12.9 7.7 %shard_map.165 = (bf16[4,4,4,384]{3,2,1,0:T(4,128)(2,1)}, bf16[2,4,4,48,384]{4,3,2,1,0:T(8,128)(2,1)S(1)}) custom-call(bf16[4,8,8,192]{3,2,1,0:T(8,128)(2,1)S(1)} %copy-done.4, bf16[4,4,4,384]{3,2,1,0:T(4,128)(2,1)S(1)} %copy-done.5, s32[1,4]{1,0:T(1,128)S(1)} %copy-done.8, s32[1,2]{1,0:T(1,128)S(1)} %copy-done.9, bf16[7,7,192]{2,1,0:T(8,128)(2,1)S(1)} %copy-done.7, ...), custom_call_target="tpu_custom_call" | custom-call | tf_op jit(solution)/shard_map/pallas_call | solution.py:283
  20.6 24.1 %shard_map.166 = f32[2,2,48,384]{3,2,1,0:T(8,128)S(1)} custom-call(bf16[2,4,4,48,384]{4,3,2,1,0:T(8,128)(2,1)S(1)} %get-tuple-element.7.halves), custom_call_target="tpu_custom_call" | custom-call | flops 1000000 | bytes 4000000 | tf_op jit(solution)/shard_map/pallas_call | solution.py:85
  44.7 0.7 %fusion = (f32[1,2,48,384]{3,2,1,0:T(8,128)}, f32[1,2,48,384]{3,2,1,0:T(8,128)S(1)}) fusion(f32[2,2,48,384]{3,2,1,0:T(8,128)S(1)} %shard_map.166), kind=kLoop, calls=%fused_computation.1 | loop fusion | bytes 589824 | tf_op jit(solution)/shard_map/slice | solution.py:298
  45.4 0.7 %fusion.1 = (f32[96,192]{1,0:T(8,128)}, f32[192,96]{0,1:T(8,128)S(1)}) fusion(f32[96,384]{1,0:T(8,128)S(1)} %bitcast.4), kind=kLoop, calls=%fused_computation.2 | loop fusion | bytes 294912 | tf_op jit(solution)/shard_map/slice | solution.py:303
  46.1 0.7 %copy.19 = f32[192,96]{1,0:T(8,128)} copy(f32[192,96]{0,1:T(8,128)S(1)} %get-tuple-element.15) | data formatting | bytes 147456
Async XLA Ops:
  3.8 1.3 %copy-start = (bf16[384,1536]{1,0:T(8,128)(2,1)S(1)}, bf16[384,1536]{1,0:T(8,128)(2,1)}, u32[]{:S(2)}) copy-start(bf16[384,1536]{1,0:T(8,128)(2,1)} %inward_two.1) | copy-start | bytes 3538948
  5.0 1.3 %copy-start.1 = (bf16[1536,384]{1,0:T(8,128)(2,1)S(1)}, bf16[1536,384]{1,0:T(8,128)(2,1)}, u32[]{:S(2)}) copy-start(bf16[1536,384]{1,0:T(8,128)(2,1)} %outward_two.1) | copy-start | bytes 3538948
  6.3 1.1 %copy-start.2 = (bf16[768,384]{1,0:T(8,128)(2,1)S(1)}, bf16[768,384]{1,0:T(8,128)(2,1)}, u32[]{:S(2)}) copy-start(bf16[768,384]{1,0:T(8,128)(2,1)} %project.1) | copy-start | bytes 1769476
  7.4 1.0 %copy-start.3 = (bf16[192,768]{1,0:T(8,128)(2,1)S(1)}, bf16[192,768]{1,0:T(8,128)(2,1)}, u32[]{:S(2)}) copy-start(bf16[192,768]{1,0:T(8,128)(2,1)} %inward_one.1) | copy-start | bytes 884740
  8.3 0.9 %copy-start.4 = (bf16[4,8,8,192]{3,2,1,0:T(8,128)(2,1)S(1)}, bf16[4,8,8,192]{3,2,1,0:T(8,128)(2,1)}, u32[]{:S(2)}) copy-start(bf16[4,8,8,192]{3,2,1,0:T(8,128)(2,1)} %feats.1) | copy-start | bytes 294916
  9.2 0.8 %copy-start.5 = (bf16[4,4,4,384]{3,2,1,0:T(4,128)(2,1)S(1)}, bf16[4,4,4,384]{3,2,1,0:T(4,128)(2,1)}, u32[]{:S(2)}) copy-start(bf16[4,4,4,384]{3,2,1,0:T(4,128)(2,1)} %cot.1) | copy-start | bytes 147460
  10.0 0.8 %copy-start.6 = (bf16[7,7,384]{2,1,0:T(8,128)(2,1)S(1)}, bf16[7,7,384]{2,1,0:T(8,128)(2,1)}, u32[]{:S(2)}) copy-start(bf16[7,7,384]{2,1,0:T(8,128)(2,1)} %kernel_two.1) | copy-start | bytes 112900
  10.8 0.7 %copy-start.7 = (bf16[7,7,192]{2,1,0:T(8,128)(2,1)S(1)}, bf16[7,7,192]{2,1,0:T(8,128)(2,1)}, u32[]{:S(2)}) copy-start(bf16[7,7,192]{2,1,0:T(8,128)(2,1)} %kernel_one.1) | copy-start | bytes 56452
  11.6 0.7 %copy-start.8 = (s32[1,4]{1,0:T(1,128)S(1)}, s32[1,4]{1,0:T(1,128)}, u32[]{:S(2)}) copy-start(s32[1,4]{1,0:T(1,128)} %keep.1) | copy-start | bytes 52
  12.2 0.7 %copy-start.9 = (s32[1,2]{1,0:T(1,128)S(1)}, s32[1,2]{1,0:T(1,128)}, u32[]{:S(2)}) copy-start(s32[1,2]{1,0:T(1,128)} %plan.1) | copy-start | bytes 28

commit v3 on v2

--- a/solution.py
+++ b/solution.py
@@ -71,10 +71,10 @@
     reps = {}
     for d in (3, 2, 1):
         reps[d] = send(put_rep, get_rep.at[d - 1], rep_sems, d - 1, rep_peer(d))
-    out[core, y] = put_rep[...].astype(jnp.float32)
+    out[core, y] = put_rep[...]
     for d in (1, 3, 2):
         reps[d].wait_recv()
-        out[(core + d) % 2, (y + d // 2) % 2] = get_rep[d - 1].astype(jnp.float32)
+        out[(core + d) % 2, (y + d // 2) % 2] = get_rep[d - 1]
     for copy in [*pairs.values(), *quads.values(), *lines.values(), *reps.values()]:
         copy.wait_send()
 
@@ -84,7 +84,7 @@
     block = halves.shape[-2:]
     return pl.pallas_call(
         functools.partial(exchange_kernel, line),
-        out_shape=jax.ShapeDtypeStruct((2, 2) + block, jnp.float32),
+        out_shape=jax.ShapeDtypeStruct((2, 2) + block, jnp.bfloat16),
         in_specs=[pl.BlockSpec(memory_space=pltpu.VMEM)],
         out_specs=pl.BlockSpec(memory_space=pltpu.VMEM),
         scratch_shapes=[
@@ -149,9 +149,19 @@
         out[i] = total
 
 
-def compute_kernel(feats, cot, keep, plan, kernel_one, gain_one, inward_one, outward_one, gain_down, project, kernel_two,
-                   gain_two, inward_two, outward_two, features, halves, pad_one, shift_one, taps_one, conv_one, expand, hidden,
-                   slope, pad_two, shift_two, taps_two, conv_two, rows_two, expand_two, hidden_two, slope_two):
+def compute_kernel(*refs):
+    count = 14
+    far, features, halves = refs[:count], refs[count], refs[count + 1]
+    near, sems = refs[count + 2:2 * count + 2], refs[2 * count + 2]
+    fetches = [pltpu.make_async_copy(far[i], near[i], sems.at[i]) for i in range(count)]
+    for i in (2, 3, 0, 4, 5, 6, 7, 8, 9, 10, 11, 12, 1, 13):
+        fetches[i].start()
+    step(*near, features, halves, *refs[2 * count + 3:], fetches)
+
+
+def step(feats, cot, keep, plan, kernel_one, gain_one, inward_one, outward_one, gain_down, project, kernel_two,
+         gain_two, inward_two, outward_two, features, halves, pad_one, shift_one, taps_one, conv_one, expand, hidden,
+                   slope, pad_two, shift_two, taps_two, conv_two, rows_two, expand_two, hidden_two, slope_two, fetches):
     tiles, side, _, narrow = feats.shape
     half = side // 2
     wide = project.shape[1]
@@ -159,22 +169,28 @@
     reach = span // 2
     rows, small = tiles * side * side, tiles * half * half
     f32, bf16 = jnp.float32, jnp.bfloat16
+    def arrive(*which):
+        for i in which:
+            fetches[i].wait()
+
+    arrive(2, 3)
     lives = []
     for t in range(tiles):
         place = sum(jnp.where(keep[0, p] == t, p, 0) for p in range(tiles))
         lives.append(jnp.where(place < plan[0, 0], 1.0, 0.0).astype(f32))
 
+    arrive(0, 4)
     for d in range(span):
         taps_one[d] = jnp.broadcast_to(kernel_one[d].astype(f32)[:, None, :], (span, 8, narrow))
-        taps_two[d] = jnp.broadcast_to(kernel_two[d].astype(f32)[:, None, :], (span, 8, wide))
     pad_one[...] = jnp.zeros_like(pad_one)
     for t in range(tiles):
         pad_one[:, t, 8:8 + side, :] = feats[t].astype(f32) * lives[t]
     for d in range(span):
         shift_one[d] = pad_one[:, :, 8 + d - reach:8 + d - reach + side, :]
     side_sum(shift_one, taps_one, conv_one, False)
+    arrive(5, 6, 7)
     unit, _ = centre_scale(conv_one[...].reshape(rows, narrow))
-    normed = (unit * gain_one[...].astype(f32)).astype(bf16)
+    normed = (unit * gain_one[...].astype(f32)[None]).astype(bf16)
     plain = pad_one[:, :, 8:8 + side, :].reshape(rows, narrow).astype(bf16)
     to = lax.broadcasted_iota(jnp.int32, (rows, rows), 0)
     column_pair, rest = to & (half - 1), to >> (half.bit_length() - 1)
@@ -186,12 +202,15 @@
     plain = dot(order, plain)
     expand[...] = dot(normed, inward_one[...])
     gelu_rows(expand, hidden, slope, 16, expand.shape[1])
-    section = (plain + dot(hidden[...], outward_one[...])).astype(bf16).astype(f32)
+    arrive(8, 9, 10, 11, 12, 1, 13)
+    section = (plain + dot(hidden[...], outward_one[...], (1, 1))).astype(bf16).astype(f32)
     unit_down, scale_down = centre_scale(section)
-    gain = gain_down[...].astype(f32)
+    gain = gain_down[...].astype(f32)[None]
     down = (unit_down * gain).astype(bf16)
     merged = sum(dot(down[q * small:(q + 1) * small], project[q * narrow:(q + 1) * narrow]) for q in range(4)).astype(bf16).astype(f32)
 
+    for d in range(span):
+        taps_two[d] = jnp.broadcast_to(kernel_two[d].astype(f32)[:, None, :], (span, 8, wide))
     lane = lax.broadcasted_iota(jnp.int32, (half, tiles * half, wide), 1) & (half - 1)
 
     def second_conv(values, flip):
@@ -205,7 +224,7 @@
         return conv_two[...].reshape(small, wide)
 
     unit_two, scale_two = centre_scale(second_conv(merged, False))
-    second_gain = gain_two[...].astype(f32)
+    second_gain = gain_two[...].astype(f32)[None]
     normed_two = (unit_two * second_gain).astype(bf16)
     expand_two[...] = dot(normed_two, inward_two[...])
     gelu_rows(expand_two, hidden_two, slope_two, 16, expand_two.shape[1] // 2)
@@ -238,7 +257,7 @@
     back_down = back_down.astype(bf16).astype(f32)
     back_section = norm_back(back_down * gain, unit_down, scale_down).astype(bf16)
     grad_outward = dot(hidden[...], back_section, (0, 0))
-    back_hidden = dot(back_section, outward_one[...], (1, 1)).astype(bf16).astype(f32)
+    back_hidden = dot(back_section, outward_one[...]).astype(bf16).astype(f32)
     back_expand = (slope[...] * back_hidden).astype(bf16)
     grad_inward = dot(back_expand, normed, (0, 0))
     put(1, 0, jnp.concatenate([grad_inward, grad_outward], axis=1))
@@ -267,6 +286,15 @@
     ]
 
 
+def finish_kernel(got, inward, outward, project):
+    part, narrow = got.shape[2], outward.shape[1]
+    both = jnp.concatenate([got[1, y].astype(jnp.float32) for y in range(2)], axis=0)
+    inward[...] = both[:, :narrow].T
+    outward[...] = both[:, narrow:]
+    for y in range(2):
+        project[y * part:(y + 1) * part] = got[0, y].astype(jnp.float32)
+
+
 def fits(slides, reps, rows):
     return reps == 4 and slides % 2 == 0 and slides > 2 and rows % (slides * 32) == 0
 
@@ -278,29 +306,37 @@
     narrow = tile_feats.shape[3]
     direct = fits(slides, reps, rows)
     cut = (4, slides // 2, rows // slides // 2) if direct else (1, 1, rows)
+    operands = (tile_feats, cotangent, keep_list, tile_plan, kernel_one, gain_one, inward_one, outward_one.T, gain_down,
+                project_down, kernel_two, gain_two, inward_two, outward_two)
+    spaces = [pltpu.SMEM if a.dtype == jnp.int32 else pltpu.VMEM for a in operands]
     whole = pl.BlockSpec(memory_space=pltpu.VMEM)
-    scalars = pl.BlockSpec(memory_space=pltpu.SMEM)
     features, halves = pl.pallas_call(
         compute_kernel,
         out_shape=(
             jax.ShapeDtypeStruct(cotangent.shape, jnp.bfloat16),
             jax.ShapeDtypeStruct((2,) + cut + (wide,), jnp.bfloat16 if direct else jnp.float32),
         ),
-        in_specs=[whole, whole, scalars, scalars] + [whole] * 10,
+        in_specs=[pl.BlockSpec(memory_space=pltpu.HBM)] * len(operands),
         out_specs=(whole, whole),
-        scratch_shapes=compute_scratch(
+        scratch_shapes=[space(a.shape, a.dtype) for space, a in zip(spaces, operands)]
+        + [pltpu.SemaphoreType.DMA((len(operands),))]
+        + compute_scratch(
             tile_feats.shape[0], tile_feats.shape[1], narrow, wide, kernel_one.shape[0], inward_one.shape[1], inward_two.shape[1]),
-        compiler_params=pltpu.CompilerParams(vmem_limit_bytes=48 * 1024 * 1024),
-    )(tile_feats, cotangent, keep_list, tile_plan, kernel_one, gain_one[None], inward_one, outward_one, gain_down[None],
-      project_down, kernel_two, gain_two[None], inward_two, outward_two)
-    if direct:
-        got = exchange(halves, slides).reshape(2, rows // slides, wide)
-        project, both = got[0], got[1]
-    else:
+        compiler_params=pltpu.CompilerParams(vmem_limit_bytes=60 * 1024 * 1024),
+    )(*operands)
+    if not direct:
         project, both = (
             lax.psum(lax.psum_scatter(g.reshape(rows, wide), "slide", scatter_dimension=0, tiled=True), "rep")
             for g in (halves[0], halves[1]))
-    return features, both[:, :narrow].T, both[:, narrow:], project
+        return features, both[:, :narrow].T, both[:, narrow:], project
+    share = rows // slides
+    inward, outward, project = pl.pallas_call(
+        finish_kernel,
+        out_shape=tuple(jax.ShapeDtypeStruct(d, jnp.float32) for d in ((narrow, share), (share, narrow), (share, wide))),
+        in_specs=[whole],
+        out_specs=(whole,) * 3,
+    )(exchange(halves, slides))
+    return features, inward, outward, project
 
 
 def solution(mesh):

time: 47.4 us -> 37.4 us (0.79)
  local copies, waits for them, and re-layouts: 14.4 us -> 1.91 us
  Pallas kernels: 31.8 us -> 34.6 us
    unnamed x22 -> x4, local copies, waits for them, and re-layouts: 11 us -> 1.91 us
    broadcast_in_dim x3 -> x0, local copies, waits for them, and re-layouts: 2 us -> none  [the longest x1 0.68 us: per_device(): gain_two[None]]
    pallas_call x0 -> x1, Pallas kernels: none -> 1.74 us  [per_device(): pl.pallas_call(finish_kernel, out_shape=tuple((jax.ShapeDtypeStruct(d, jn...]
    slice x2 -> x0, local copies, waits for them, and re-layouts: 1.42 us -> none  [the longest x1 0.73 us: per_device(): return (features, both[:, :narrow].T, both[:, narrow:], project)]
    pallas_call x1, Pallas kernels: 7.7 us -> 8.84 us  [per_device(): pl.pallas_call(compute_kernel, out_shape=(jax.ShapeDtypeStruct(cotangent....]
where the time goes in v3:
time: 37.4 us; the launch traced here: 37.2 us
  Pallas kernels  34.6 us (93%)
  local copies, waits for them, and re-layouts  1.91 us (5%)
  between operations  0.67 us (2%)
    pallas_call x1, Pallas kernels, exchange(): pl.pallas_call(functools.partial(exchange_kernel, line), out_shape=jax.Sh...  24 us
    pallas_call x1, Pallas kernels, per_device(): pl.pallas_call(compute_kernel, out_shape=(jax.ShapeDtypeStruct(cotangent....  8.84 us
    unnamed x4, local copies, waits for them, and re-layouts  1.91 us
    pallas_call x1, Pallas kernels, per_device(): pl.pallas_call(finish_kernel, out_shape=tuple((jax.ShapeDtypeStruct(d, jn...  1.74 us

profile of v3, /device:TPU:0, one launch (start us, length us, event | category | flops | bytes accessed | tf_op | source)
XLA Modules:
  0.0 37.2 jit_solution(9863135925967528215)
XLA Ops:
  0.6 8.8 %shard_map.165 = (bf16[4,4,4,384]{3,2,1,0:T(4,128)(2,1)}, bf16[2,4,4,48,384]{4,3,2,1,0:T(8,128)(2,1)}) custom-call(bf16[4,8,8,192]{3,2,1,0:T(8,128)(2,1)} %refs_0_.1, bf16[4,4,4,384]{3,2,1,0:T(4,128)(2,1)} %refs_1_.1, s32[1,4]{1,0:T(1,128)} %refs_2_.1, s32[1,2]{1,0:T(1,128)} %refs_3_.1, bf16[7,7,192]{2,1,0:T(8,128)(2,1)} %refs_4_.1, bf16[192]{0:T(256)(128)(2,1)} %refs_5_.1, ...), custom_call_target="tpu_custom_call" | custom-call | tf_op jit(solution)/shard_map/pallas_call | solution.py:313
  9.5 0.0 copy-start
  9.5 1.3 %copy-done = bf16[2,4,4,48,384]{4,3,2,1,0:T(8,128)(2,1)S(1)} copy-done((bf16[2,4,4,48,384]{4,3,2,1,0:T(8,128)(2,1)S(1)}, bf16[2,4,4,48,384]{4,3,2,1,0:T(8,128)(2,1)}, u32[]{:S(2)}) %copy-start) | copy-done | bytes 1179672
  10.8 24.0 %shard_map.166.got = bf16[2,2,48,384]{3,2,1,0:T(8,128)(2,1)S(1)} custom-call(bf16[2,4,4,48,384]{4,3,2,1,0:T(8,128)(2,1)S(1)} %copy-done), custom_call_target="tpu_custom_call" | custom-call | flops 1000000 | bytes 4000000 | tf_op jit(solution)/shard_map/pallas_call | solution.py:85
  34.8 0.0 copy-start.1
  34.8 0.6 %copy-done.1 = bf16[2,2,48,384]{3,2,1,0:T(8,128)(2,1)} copy-done((bf16[2,2,48,384]{3,2,1,0:T(8,128)(2,1)}, bf16[2,2,48,384]{3,2,1,0:T(8,128)(2,1)S(1)}, u32[]{:S(2)}) %copy-start.1) | copy-done | bytes 147480
  35.5 1.7 %shard_map.167 = (f32[192,96]{1,0:T(8,128)}, f32[96,192]{1,0:T(8,128)}, f32[96,384]{1,0:T(8,128)}) custom-call(bf16[2,2,48,384]{3,2,1,0:T(8,128)(2,1)} %copy-done.1), custom_call_target="tpu_custom_call" | custom-call | tf_op jit(solution)/shard_map/pallas_call | solution.py:333
Async XLA Ops:
  9.5 1.3 %copy-start = (bf16[2,4,4,48,384]{4,3,2,1,0:T(8,128)(2,1)S(1)}, bf16[2,4,4,48,384]{4,3,2,1,0:T(8,128)(2,1)}, u32[]{:S(2)}) copy-start(bf16[2,4,4,48,384]{4,3,2,1,0:T(8,128)(2,1)} %get-tuple-element.10.halves) | copy-start | bytes 3538948
  34.8 0.7 %copy-start.1 = (bf16[2,2,48,384]{3,2,1,0:T(8,128)(2,1)}, bf16[2,2,48,384]{3,2,1,0:T(8,128)(2,1)S(1)}, u32[]{:S(2)}) copy-start(bf16[2,2,48,384]{3,2,1,0:T(8,128)(2,1)S(1)} %shard_map.166.got) | copy-start | bytes 442372

commit v4 on v3

--- a/solution.py
+++ b/solution.py
@@ -10,13 +10,16 @@
 MESH = pl.DeviceIdType.MESH
 
 
-def exchange_kernel(line, halves, out, get_pair, put_quad, get_quad, mine, put_line, get_line, put_rep, get_rep, pair_sems, quad_sems, line_sems, rep_sems):
+def exchange_kernel(line, halves, out, own, get_pair, put_sq, get_sq, put_ln, get_ln, mine_a, mine_b, put_a, get_a, put_b, get_b,
+                    put_rep, get_rep, own_sem, pair_sems, sq_sems, ln_sems, a_sems, b_sems, rep_sems):
     s = lax.axis_index("slide")
     r = lax.axis_index("rep")
     core, y = r % 2, r // 2
     x, z = s % 2, s // 2
-    spot = x * 2 + y
+    cut = put_sq.shape[-1]
     pair_peer = (s, y * 2 + 1 - core)
+    own_copy = pltpu.make_async_copy(halves.at[core], own, own_sem)
+    own_copy.start()
 
     def quad_peer(d):
         return (z * 2 + (x + d // 2) % 2, ((y + d) % 2) * 2 + core)
@@ -35,73 +38,101 @@
     for peer in peers:
         pl.semaphore_signal(barrier, inc=1, device_id=peer, device_id_type=MESH)
     pl.semaphore_wait(barrier, len(peers))
+    started = []
 
     def send(src, dst, sems, slot, peer):
         copy = pltpu.make_async_remote_copy(
             src_ref=src, dst_ref=dst, send_sem=sems.at[0, slot], recv_sem=sems.at[1, slot],
             device_id=peer, device_id_type=MESH)
         copy.start()
+        started.append(copy)
         return copy
 
-    pairs = {}
+    def wide(value):
+        return value.astype(jnp.float32)
+
+    others = range(line - 1, 0, -1)
+    pairs = {d: send(halves.at[1 - core, quad_spot(d)], get_pair.at[d], pair_sems, d, pair_peer) for d in (3, 2, 1, 0)}
+    own_copy.wait()
+    squares, lines = {}, {}
     for d in (3, 2, 1, 0):
-        pairs[d] = send(halves.at[1 - core, quad_spot(d)], get_pair.at[d], pair_sems, d, pair_peer)
-    quads = {}
-    for d in (3, 2, 1):
         pairs[d].wait_recv()
-        put_quad[d - 1] = (halves[core, quad_spot(d)].astype(jnp.float32) + get_pair[d].astype(jnp.float32)).astype(jnp.bfloat16)
-        quads[d] = send(put_quad.at[d - 1], get_quad.at[d - 1], quad_sems, d - 1, quad_peer(d))
-    pairs[0].wait_recv()
-    mine[...] = halves[core, spot].astype(jnp.float32) + get_pair[0].astype(jnp.float32)
+        q = quad_spot(d)
+        first = wide(own[q, :, :, :cut]) + wide(get_pair[d, :, :, :cut])
+        if d:
+            put_sq[d - 1] = first.astype(jnp.bfloat16)
+            squares[d] = send(put_sq.at[d - 1], get_sq.at[d - 1], sq_sems, d - 1, quad_peer(d))
+        else:
+            mine_a[...] = first
+        for e in (*others, 0):
+            at = (z + e) % line
+            last = wide(own[q, at, :, cut:]) + wide(get_pair[d, at, :, cut:])
+            if e:
+                put_ln[e - 1, q] = last.astype(jnp.bfloat16)
+            else:
+                mine_b[q] = last
+    for e in others:
+        lines[e] = send(put_ln.at[e - 1], get_ln.at[e - 1], ln_sems, e - 1, line_peer(e))
+    for d in squares:
+        squares[d].wait_recv()
+    then = []
+    for e in (*others, 0):
+        at = (z + e) % line
+        total_a = mine_a[at] + wide(get_sq[0, at]) + wide(get_sq[1, at]) + wide(get_sq[2, at])
+        if e:
+            put_a[e - 1] = total_a.astype(jnp.bfloat16)
+            then.append(send(put_a.at[e - 1], get_a.at[e - 1], a_sems, e - 1, line_peer(e)))
+    for e in lines:
+        lines[e].wait_recv()
+    for d in (3, 2, 1, 0):
+        q = quad_spot(d)
+        total_b = mine_b[q]
+        for e in others:
+            total_b = total_b + wide(get_ln[e - 1, q])
+        if d:
+            put_b[d - 1] = total_b.astype(jnp.bfloat16)
+            then.append(send(put_b.at[d - 1], get_b.at[d - 1], b_sems, d - 1, quad_peer(d)))
+    for copy in then:
+        copy.wait_recv()
+    for e in others:
+        total_a = total_a + wide(get_a[e - 1])
     for d in (1, 2, 3):
-        quads[d].wait_recv()
-    lines = {}
-    for d in [*range(line - 1, 0, -1), 0]:
-        at = (z + d) % line
-        part = mine[at] + get_quad[0, at].astype(jnp.float32) + get_quad[1, at].astype(jnp.float32) + get_quad[2, at].astype(jnp.float32)
-        if d:
-            put_line[d - 1] = part.astype(jnp.bfloat16)
-            lines[d] = send(put_line.at[d - 1], get_line.at[d - 1], line_sems, d - 1, line_peer(d))
-        else:
-            total = part
-    for d in range(1, line):
-        lines[d].wait_recv()
-        total = total + get_line[d - 1].astype(jnp.float32)
-    put_rep[...] = total.astype(jnp.bfloat16)
-    reps = {}
-    for d in (3, 2, 1):
-        reps[d] = send(put_rep, get_rep.at[d - 1], rep_sems, d - 1, rep_peer(d))
+        total_b = total_b + wide(get_b[d - 1])
+    put_rep[:, :cut] = total_a.astype(jnp.bfloat16)
+    put_rep[:, cut:] = total_b.astype(jnp.bfloat16)
+    reps = {d: send(put_rep, get_rep.at[d - 1], rep_sems, d - 1, rep_peer(d)) for d in (3, 2, 1)}
     out[core, y] = put_rep[...]
     for d in (1, 3, 2):
         reps[d].wait_recv()
         out[(core + d) % 2, (y + d // 2) % 2] = get_rep[d - 1]
-    for copy in [*pairs.values(), *quads.values(), *lines.values(), *reps.values()]:
+    for copy in started:
         copy.wait_send()
 
 
 def exchange(halves, slides):
     line = slides // 2
-    block = halves.shape[-2:]
+    part, width = halves.shape[-2:]
+    cut = width // 3 * 2
+    first, last, block = (part, cut), (part, width - cut), (part, width)
+    bf16, f32 = jnp.bfloat16, jnp.float32
+    buffers = [
+        ((4, line) + block, bf16), ((4, line) + block, bf16),
+        ((3, line) + first, bf16), ((3, line) + first, bf16),
+        ((line - 1, 4) + last, bf16), ((line - 1, 4) + last, bf16),
+        ((line,) + first, f32), ((4,) + last, f32),
+        ((line - 1,) + first, bf16), ((line - 1,) + first, bf16),
+        ((3,) + last, bf16), ((3,) + last, bf16),
+        (block, bf16), ((3,) + block, bf16),
+    ]
+    slots = (4, 3, line - 1, line - 1, 3, 3)
     return pl.pallas_call(
         functools.partial(exchange_kernel, line),
-        out_shape=jax.ShapeDtypeStruct((2, 2) + block, jnp.bfloat16),
-        in_specs=[pl.BlockSpec(memory_space=pltpu.VMEM)],
+        out_shape=jax.ShapeDtypeStruct((2, 2) + block, bf16),
+        in_specs=[pl.BlockSpec(memory_space=pl.ANY)],
         out_specs=pl.BlockSpec(memory_space=pltpu.VMEM),
-        scratch_shapes=[
-            pltpu.VMEM((4, line) + block, jnp.bfloat16),
-            pltpu.VMEM((3, line) + block, jnp.bfloat16),
-            pltpu.VMEM((3, line) + block, jnp.bfloat16),
-            pltpu.VMEM((line,) + block, jnp.float32),
-            pltpu.VMEM((line - 1,) + block, jnp.bfloat16),
-            pltpu.VMEM((line - 1,) + block, jnp.bfloat16),
-            pltpu.VMEM(block, jnp.bfloat16),
-            pltpu.VMEM((3,) + block, jnp.bfloat16),
-            pltpu.SemaphoreType.DMA((2, 4)),
-            pltpu.SemaphoreType.DMA((2, 3)),
-            pltpu.SemaphoreType.DMA((2, line - 1)),
-            pltpu.SemaphoreType.DMA((2, 3)),
-        ],
-        compiler_params=pltpu.CompilerParams(collective_id=0, has_side_effects=True, vmem_limit_bytes=48 * 1024 * 1024),
+        scratch_shapes=[pltpu.VMEM(*b) for b in buffers]
+        + [pltpu.SemaphoreType.DMA] + [pltpu.SemaphoreType.DMA((2, n)) for n in slots],
+        compiler_params=pltpu.CompilerParams(collective_id=0, has_side_effects=True, vmem_limit_bytes=60 * 1024 * 1024),
         cost_estimate=pl.CostEstimate(flops=10**6, bytes_accessed=4 * 10**6, transcendentals=0),
     )(halves)
 
@@ -295,8 +326,8 @@
         project[y * part:(y + 1) * part] = got[0, y].astype(jnp.float32)
 
 
-def fits(slides, reps, rows):
-    return reps == 4 and slides % 2 == 0 and slides > 2 and rows % (slides * 32) == 0
+def fits(slides, reps, rows, wide):
+    return wide % 384 == 0 and reps == 4 and slides % 2 == 0 and slides > 2 and rows % (slides * 32) == 0
 
 
 def per_device(tile_feats, cotangent, keep_list, tile_plan, kernel_one, gain_one, inward_one, outward_one, gain_down,
@@ -304,7 +335,7 @@
     slides, reps = lax.axis_size("slide"), lax.axis_size("rep")
     rows, wide = project_down.shape
     narrow = tile_feats.shape[3]
-    direct = fits(slides, reps, rows)
+    direct = fits(slides, reps, rows, wide)
     cut = (4, slides // 2, rows // slides // 2) if direct else (1, 1, rows)
     operands = (tile_feats, cotangent, keep_list, tile_plan, kernel_one, gain_one, inward_one, outward_one.T, gain_down,
                 project_down, kernel_two, gain_two, inward_two, outward_two)
@@ -335,6 +366,7 @@
         out_shape=tuple(jax.ShapeDtypeStruct(d, jnp.float32) for d in ((narrow, share), (share, narrow), (share, wide))),
         in_specs=[whole],
         out_specs=(whole,) * 3,
+        compiler_params=pltpu.CompilerParams(vmem_limit_bytes=60 * 1024 * 1024),
     )(exchange(halves, slides))
     return features, inward, outward, project
 

time: 37.4 us -> 33.6 us (0.90)
  local copies, waits for them, and re-layouts: 1.91 us -> 0 us
  Pallas kernels: 34.6 us -> 32.8 us
    unnamed x4 -> x0, local copies, waits for them, and re-layouts: 1.91 us -> none
    pallas_call x1, Pallas kernels: 24 us -> 22.2 us  [exchange(): pl.pallas_call(functools.partial(exchange_kernel, line), out_shape=jax.Sh...]
where the time goes in v4:
time: 33.6 us; the launch traced here: 33.4 us
  Pallas kernels  32.8 us (98%)
  between operations  0.65 us (2%)
    pallas_call x1, Pallas kernels, exchange(): pl.pallas_call(functools.partial(exchange_kernel, line), out_shape=jax.Sh...  22.2 us
    pallas_call x1, Pallas kernels, per_device(): pl.pallas_call(compute_kernel, out_shape=(jax.ShapeDtypeStruct(cotangent....  8.83 us
    pallas_call x1, Pallas kernels, per_device(): pl.pallas_call(finish_kernel, out_shape=tuple((jax.ShapeDtypeStruct(d, jn...  1.74 us

profile of v4, /device:TPU:0, one launch (start us, length us, event | category | flops | bytes accessed | tf_op | source)
XLA Modules:
  0.0 33.4 jit_solution(4787069406321902480)
XLA Ops:
  0.6 8.8 %shard_map.165 = (bf16[4,4,4,384]{3,2,1,0:T(4,128)(2,1)}, bf16[2,4,4,48,384]{4,3,2,1,0:T(8,128)(2,1)}) custom-call(bf16[4,8,8,192]{3,2,1,0:T(8,128)(2,1)} %refs_0_.1, bf16[4,4,4,384]{3,2,1,0:T(4,128)(2,1)} %refs_1_.1, s32[1,4]{1,0:T(1,128)} %refs_2_.1, s32[1,2]{1,0:T(1,128)} %refs_3_.1, bf16[7,7,192]{2,1,0:T(8,128)(2,1)} %refs_4_.1, bf16[192]{0:T(256)(128)(2,1)} %refs_5_.1, ...), custom_call_target="tpu_custom_call" | custom-call | tf_op jit(solution)/shard_map/pallas_call | solution.py:344
  9.5 22.2 %shard_map.166.got = bf16[2,2,48,384]{3,2,1,0:T(8,128)(2,1)} custom-call(bf16[2,4,4,48,384]{4,3,2,1,0:T(8,128)(2,1)} %get-tuple-element.10.halves), custom_call_target="tpu_custom_call" | custom-call | flops 1000000 | bytes 4000000 | tf_op jit(solution)/shard_map/pallas_call | solution.py:128
  31.7 1.7 %shard_map.167 = (f32[192,96]{1,0:T(8,128)}, f32[96,192]{1,0:T(8,128)}, f32[96,384]{1,0:T(8,128)}) custom-call(bf16[2,2,48,384]{3,2,1,0:T(8,128)(2,1)} %shard_map.166.got), custom_call_target="tpu_custom_call" | custom-call | tf_op jit(solution)/shard_map/pallas_call | solution.py:364

commit v5 on v4

--- a/solution.py
+++ b/solution.py
@@ -10,34 +10,47 @@
 MESH = pl.DeviceIdType.MESH
 
 
-def exchange_kernel(line, halves, out, own, get_pair, put_sq, get_sq, put_ln, get_ln, mine_a, mine_b, put_a, get_a, put_b, get_b,
-                    put_rep, get_rep, own_sem, pair_sems, sq_sems, ln_sems, a_sems, b_sems, rep_sems):
+def routes(line):
+    s = lax.axis_index("slide")
+    r = lax.axis_index("rep")
+    core, y = r % 2, r // 2
+    x, z = s % 2, s // 2
+
+    def quad_peer(d):
+        return (z * 2 + (x + d // 2) % 2, ((y + d) % 2) * 2 + core)
+
+    def line_peer(d):
+        return (((z + d) % line) * 2 + x, r)
+
+    def rep_peer(d):
+        return (s, ((y + d // 2) % 2) * 2 + (core + d) % 2)
+
+    return quad_peer, line_peer, rep_peer
+
+
+def greet(line):
+    quad_peer, line_peer, rep_peer = routes(line)
+    barrier = pltpu.get_barrier_semaphore()
+    peers = [rep_peer(d) for d in (1, 2, 3)] + [quad_peer(d) for d in (2, 3)] + [line_peer(d) for d in range(1, line)]
+    for peer in peers:
+        pl.semaphore_signal(barrier, inc=1, device_id=peer, device_id_type=MESH)
+
+
+def exchange_part(line, halves, out, get_pair, put_sq, get_sq, put_ln, get_ln, mine_a, mine_b, put_a, get_a, put_b, get_b,
+                    put_rep, get_rep, pair_sems, sq_sems, ln_sems, a_sems, b_sems, rep_sems):
     s = lax.axis_index("slide")
     r = lax.axis_index("rep")
     core, y = r % 2, r // 2
     x, z = s % 2, s // 2
     cut = put_sq.shape[-1]
     pair_peer = (s, y * 2 + 1 - core)
-    own_copy = pltpu.make_async_copy(halves.at[core], own, own_sem)
-    own_copy.start()
-
-    def quad_peer(d):
-        return (z * 2 + (x + d // 2) % 2, ((y + d) % 2) * 2 + core)
-
-    def line_peer(d):
-        return (((z + d) % line) * 2 + x, r)
-
-    def rep_peer(d):
-        return (s, ((y + d // 2) % 2) * 2 + (core + d) % 2)
+
+    quad_peer, line_peer, rep_peer = routes(line)
 
     def quad_spot(d):
         return ((x + d // 2) % 2) * 2 + (y + d) % 2
 
-    barrier = pltpu.get_barrier_semaphore()
-    peers = [rep_peer(d) for d in (1, 2, 3)] + [quad_peer(d) for d in (2, 3)] + [line_peer(d) for d in range(1, line)]
-    for peer in peers:
-        pl.semaphore_signal(barrier, inc=1, device_id=peer, device_id_type=MESH)
-    pl.semaphore_wait(barrier, len(peers))
+    pl.semaphore_wait(pltpu.get_barrier_semaphore(), line + 4)
     started = []
 
     def send(src, dst, sems, slot, peer):
@@ -53,12 +66,11 @@
 
     others = range(line - 1, 0, -1)
     pairs = {d: send(halves.at[1 - core, quad_spot(d)], get_pair.at[d], pair_sems, d, pair_peer) for d in (3, 2, 1, 0)}
-    own_copy.wait()
     squares, lines = {}, {}
     for d in (3, 2, 1, 0):
         pairs[d].wait_recv()
         q = quad_spot(d)
-        first = wide(own[q, :, :, :cut]) + wide(get_pair[d, :, :, :cut])
+        first = wide(halves[core, q, :, :, :cut]) + wide(get_pair[d, :, :, :cut])
         if d:
             put_sq[d - 1] = first.astype(jnp.bfloat16)
             squares[d] = send(put_sq.at[d - 1], get_sq.at[d - 1], sq_sems, d - 1, quad_peer(d))
@@ -66,7 +78,7 @@
             mine_a[...] = first
         for e in (*others, 0):
             at = (z + e) % line
-            last = wide(own[q, at, :, cut:]) + wide(get_pair[d, at, :, cut:])
+            last = wide(halves[core, q, at, :, cut:]) + wide(get_pair[d, at, :, cut:])
             if e:
                 put_ln[e - 1, q] = last.astype(jnp.bfloat16)
             else:
@@ -109,14 +121,12 @@
         copy.wait_send()
 
 
-def exchange(halves, slides):
-    line = slides // 2
-    part, width = halves.shape[-2:]
+def exchange_scratch(line, part, width):
     cut = width // 3 * 2
     first, last, block = (part, cut), (part, width - cut), (part, width)
     bf16, f32 = jnp.bfloat16, jnp.float32
     buffers = [
-        ((4, line) + block, bf16), ((4, line) + block, bf16),
+        ((2, 4, line) + block, bf16), ((4, line) + block, bf16),
         ((3, line) + first, bf16), ((3, line) + first, bf16),
         ((line - 1, 4) + last, bf16), ((line - 1, 4) + last, bf16),
         ((line,) + first, f32), ((4,) + last, f32),
@@ -124,17 +134,7 @@
         ((3,) + last, bf16), ((3,) + last, bf16),
         (block, bf16), ((3,) + block, bf16),
     ]
-    slots = (4, 3, line - 1, line - 1, 3, 3)
-    return pl.pallas_call(
-        functools.partial(exchange_kernel, line),
-        out_shape=jax.ShapeDtypeStruct((2, 2) + block, bf16),
-        in_specs=[pl.BlockSpec(memory_space=pl.ANY)],
-        out_specs=pl.BlockSpec(memory_space=pltpu.VMEM),
-        scratch_shapes=[pltpu.VMEM(*b) for b in buffers]
-        + [pltpu.SemaphoreType.DMA] + [pltpu.SemaphoreType.DMA((2, n)) for n in slots],
-        compiler_params=pltpu.CompilerParams(collective_id=0, has_side_effects=True, vmem_limit_bytes=60 * 1024 * 1024),
-        cost_estimate=pl.CostEstimate(flops=10**6, bytes_accessed=4 * 10**6, transcendentals=0),
-    )(halves)
+    return [pltpu.VMEM(*b) for b in buffers] + [pltpu.SemaphoreType.DMA((2, n)) for n in (4, 3, line - 1, line - 1, 3, 3)]
 
 
 def dot(a, b, contract=(1, 0)):
@@ -180,14 +180,27 @@
         out[i] = total
 
 
-def compute_kernel(*refs):
-    count = 14
+def fetch(far, near, sems):
+    fetches = [pltpu.make_async_copy(far[i], near[i], sems.at[i]) for i in range(len(far))]
+    for i in (2, 3, 0, 4, 5, 6, 7, 8, 9, 10, 11, 12, 1, 13):
+        fetches[i].start()
+    return fetches
+
+
+def compute_kernel(count, *refs):
     far, features, halves = refs[:count], refs[count], refs[count + 1]
     near, sems = refs[count + 2:2 * count + 2], refs[2 * count + 2]
-    fetches = [pltpu.make_async_copy(far[i], near[i], sems.at[i]) for i in range(count)]
-    for i in (2, 3, 0, 4, 5, 6, 7, 8, 9, 10, 11, 12, 1, 13):
-        fetches[i].start()
-    step(*near, features, halves, *refs[2 * count + 3:], fetches)
+    step(*near, features, halves, *refs[2 * count + 3:], fetch(far, near, sems))
+
+
+def whole_kernel(count, line, *refs):
+    far, features, got = refs[:count], refs[count], refs[count + 1]
+    near, sems = refs[count + 2:2 * count + 2], refs[2 * count + 2]
+    inner, (halves, *buffers) = refs[2 * count + 3:2 * count + 18], refs[2 * count + 18:]
+    fetches = fetch(far, near, sems)
+    greet(line)
+    step(*near, features, halves, *inner, fetches)
+    exchange_part(line, halves, got, *buffers)
 
 
 def step(feats, cot, keep, plan, kernel_one, gain_one, inward_one, outward_one, gain_down, project, kernel_two,
@@ -317,7 +330,8 @@
     ]
 
 
-def finish_kernel(got, inward, outward, project):
+def finish_kernel(early, got, features, inward, outward, project):
+    features[...] = early[...]
     part, narrow = got.shape[2], outward.shape[1]
     both = jnp.concatenate([got[1, y].astype(jnp.float32) for y in range(2)], axis=0)
     inward[...] = both[:, :narrow].T
@@ -336,39 +350,46 @@
     rows, wide = project_down.shape
     narrow = tile_feats.shape[3]
     direct = fits(slides, reps, rows, wide)
-    cut = (4, slides // 2, rows // slides // 2) if direct else (1, 1, rows)
     operands = (tile_feats, cotangent, keep_list, tile_plan, kernel_one, gain_one, inward_one, outward_one.T, gain_down,
                 project_down, kernel_two, gain_two, inward_two, outward_two)
     spaces = [pltpu.SMEM if a.dtype == jnp.int32 else pltpu.VMEM for a in operands]
     whole = pl.BlockSpec(memory_space=pltpu.VMEM)
-    features, halves = pl.pallas_call(
-        compute_kernel,
-        out_shape=(
-            jax.ShapeDtypeStruct(cotangent.shape, jnp.bfloat16),
-            jax.ShapeDtypeStruct((2,) + cut + (wide,), jnp.bfloat16 if direct else jnp.float32),
-        ),
-        in_specs=[pl.BlockSpec(memory_space=pltpu.HBM)] * len(operands),
-        out_specs=(whole, whole),
-        scratch_shapes=[space(a.shape, a.dtype) for space, a in zip(spaces, operands)]
+    scratch = (
+        [space(a.shape, a.dtype) for space, a in zip(spaces, operands)]
         + [pltpu.SemaphoreType.DMA((len(operands),))]
         + compute_scratch(
-            tile_feats.shape[0], tile_feats.shape[1], narrow, wide, kernel_one.shape[0], inward_one.shape[1], inward_two.shape[1]),
-        compiler_params=pltpu.CompilerParams(vmem_limit_bytes=60 * 1024 * 1024),
-    )(*operands)
+            tile_feats.shape[0], tile_feats.shape[1], narrow, wide, kernel_one.shape[0], inward_one.shape[1], inward_two.shape[1]))
+    far = [pl.BlockSpec(memory_space=pl.ANY)] * len(operands)
+    kept = jax.ShapeDtypeStruct(cotangent.shape, jnp.bfloat16)
     if not direct:
+        features, halves = pl.pallas_call(
+            functools.partial(compute_kernel, len(operands)),
+            out_shape=(kept, jax.ShapeDtypeStruct((2, 1, 1, rows, wide), jnp.float32)),
+            in_specs=far,
+            out_specs=(whole, whole),
+            scratch_shapes=scratch,
+            compiler_params=pltpu.CompilerParams(vmem_limit_bytes=60 * 1024 * 1024),
+        )(*operands)
         project, both = (
             lax.psum(lax.psum_scatter(g.reshape(rows, wide), "slide", scatter_dimension=0, tiled=True), "rep")
             for g in (halves[0], halves[1]))
         return features, both[:, :narrow].T, both[:, narrow:], project
-    share = rows // slides
-    inward, outward, project = pl.pallas_call(
+    line, share = slides // 2, rows // slides
+    features, got = pl.pallas_call(
+        functools.partial(whole_kernel, len(operands), line),
+        out_shape=(kept, jax.ShapeDtypeStruct((2, 2, share // 2, wide), jnp.bfloat16)),
+        in_specs=far,
+        out_specs=(whole, whole),
+        scratch_shapes=scratch + exchange_scratch(line, share // 2, wide),
+        compiler_params=pltpu.CompilerParams(collective_id=0, has_side_effects=True, vmem_limit_bytes=60 * 1024 * 1024),
+    )(*operands)
+    return pl.pallas_call(
         finish_kernel,
-        out_shape=tuple(jax.ShapeDtypeStruct(d, jnp.float32) for d in ((narrow, share), (share, narrow), (share, wide))),
-        in_specs=[whole],
-        out_specs=(whole,) * 3,
+        out_shape=(kept,) + tuple(jax.ShapeDtypeStruct(d, jnp.float32) for d in ((narrow, share), (share, narrow), (share, wide))),
+        in_specs=[whole] * 2,
+        out_specs=(whole,) * 4,
         compiler_params=pltpu.CompilerParams(vmem_limit_bytes=60 * 1024 * 1024),
-    )(exchange(halves, slides))
-    return features, inward, outward, project
+    )(features, got)
 
 
 def solution(mesh):

time: 33.6 us -> 30.9 us (0.920)
  Pallas kernels: 32.8 us -> 30.1 us
    pallas_call x3 -> x2, Pallas kernels: 32.8 us -> 30.1 us  [the longest x1 28.3 us: per_device(): pl.pallas_call(functools.partial(whole_kernel, len(operands), line), out_...]
where the time goes in v5:
time: 30.9 us; the launch traced here: 30.7 us
  Pallas kernels  30.1 us (97%)
  between operations  0.64 us (2%)
    pallas_call x1, Pallas kernels, per_device(): pl.pallas_call(functools.partial(whole_kernel, len(operands), line), out_...  28.3 us
    pallas_call x1, Pallas kernels, per_device(): pl.pallas_call(finish_kernel, out_shape=(kept,) + tuple((jax.ShapeDtypeSt...  1.73 us

profile of v5, /device:TPU:0, one launch (start us, length us, event | category | flops | bytes accessed | tf_op | source)
XLA Modules:
  0.0 30.7 jit_solution(8763960823910920915)
XLA Ops:
  0.6 28.3 %shard_map.165 = (bf16[4,4,4,384]{3,2,1,0:T(4,128)(2,1)}, bf16[2,2,48,384]{3,2,1,0:T(8,128)(2,1)}) custom-call(bf16[4,8,8,192]{3,2,1,0:T(8,128)(2,1)} %refs_0_.1, bf16[4,4,4,384]{3,2,1,0:T(4,128)(2,1)} %refs_1_.1, s32[1,4]{1,0:T(1,128)} %refs_2_.1, s32[1,2]{1,0:T(1,128)} %refs_3_.1, bf16[7,7,192]{2,1,0:T(8,128)(2,1)} %refs_4_.1, bf16[192]{0:T(256)(128)(2,1)} %refs_5_.1, ...), custom_call_target="tpu_custom_call" | custom-call | tf_op jit(solution)/shard_map/pallas_call | solution.py:378
  29.0 1.7 %shard_map.166 = (bf16[4,4,4,384]{3,2,1,0:T(4,128)(2,1)}, f32[192,96]{1,0:T(8,128)}, f32[96,192]{1,0:T(8,128)}, f32[96,384]{1,0:T(8,128)}) custom-call(bf16[4,4,4,384]{3,2,1,0:T(4,128)(2,1)} %get-tuple-element.6.early, bf16[2,2,48,384]{3,2,1,0:T(8,128)(2,1)} %get-tuple-element.7.got), custom_call_target="tpu_custom_call" | custom-call | tf_op jit(solution)/shard_map/pallas_call | solution.py:386

commit v6 on v5

--- a/solution.py
+++ b/solution.py
@@ -81,10 +81,9 @@
             last = wide(halves[core, q, at, :, cut:]) + wide(get_pair[d, at, :, cut:])
             if e:
                 put_ln[e - 1, q] = last.astype(jnp.bfloat16)
+                lines[e, d] = send(put_ln.at[e - 1, q], get_ln.at[e - 1, q], ln_sems, (e - 1) * 4 + d, line_peer(e))
             else:
                 mine_b[q] = last
-    for e in others:
-        lines[e] = send(put_ln.at[e - 1], get_ln.at[e - 1], ln_sems, e - 1, line_peer(e))
     for d in squares:
         squares[d].wait_recv()
     then = []
@@ -134,7 +133,7 @@
         ((3,) + last, bf16), ((3,) + last, bf16),
         (block, bf16), ((3,) + block, bf16),
     ]
-    return [pltpu.VMEM(*b) for b in buffers] + [pltpu.SemaphoreType.DMA((2, n)) for n in (4, 3, line - 1, line - 1, 3, 3)]
+    return [pltpu.VMEM(*b) for b in buffers] + [pltpu.SemaphoreType.DMA((2, n)) for n in (4, 3, 4 * (line - 1), line - 1, 3, 3)]
 
 
 def dot(a, b, contract=(1, 0)):

time: 30.9 us -> 31 us (level)
  no operation moved by 1% of the time
where the time goes in v6:
time: 31 us; the launch traced here: 30.9 us
  Pallas kernels  30.2 us (97%)
  between operations  0.64 us (2%)
    pallas_call x1, Pallas kernels, per_device(): pl.pallas_call(functools.partial(whole_kernel, len(operands), line), out_...  28.5 us
    pallas_call x1, Pallas kernels, per_device(): pl.pallas_call(finish_kernel, out_shape=(kept,) + tuple((jax.ShapeDtypeSt...  1.73 us

profile of v6, /device:TPU:0, one launch (start us, length us, event | category | flops | bytes accessed | tf_op | source)
XLA Modules:
  0.0 30.9 jit_solution(12018576273069936964)
XLA Ops:
  0.6 28.5 %shard_map.165 = (bf16[4,4,4,384]{3,2,1,0:T(4,128)(2,1)}, bf16[2,2,48,384]{3,2,1,0:T(8,128)(2,1)}) custom-call(bf16[4,8,8,192]{3,2,1,0:T(8,128)(2,1)} %refs_0_.1, bf16[4,4,4,384]{3,2,1,0:T(4,128)(2,1)} %refs_1_.1, s32[1,4]{1,0:T(1,128)} %refs_2_.1, s32[1,2]{1,0:T(1,128)} %refs_3_.1, bf16[7,7,192]{2,1,0:T(8,128)(2,1)} %refs_4_.1, bf16[192]{0:T(256)(128)(2,1)} %refs_5_.1, ...), custom_call_target="tpu_custom_call" | custom-call | tf_op jit(solution)/shard_map/pallas_call | solution.py:377
  29.2 1.7 %shard_map.166 = (bf16[4,4,4,384]{3,2,1,0:T(4,128)(2,1)}, f32[192,96]{1,0:T(8,128)}, f32[96,192]{1,0:T(8,128)}, f32[96,384]{1,0:T(8,128)}) custom-call(bf16[4,4,4,384]{3,2,1,0:T(4,128)(2,1)} %get-tuple-element.6.early, bf16[2,2,48,384]{3,2,1,0:T(8,128)(2,1)} %get-tuple-element.7.got), custom_call_target="tpu_custom_call" | custom-call | tf_op jit(solution)/shard_map/pallas_call | solution.py:385
